TPU v7x, 512 devices: a whole 4x8x8 slice. The times are simulated.
512 devices in a mesh: ctx: 64 (over x, y_lo, z), cand: 8 (over y_hi, core).
Axes of the slice: x: 4, y: 8 (y_hi: 4, y_lo: 2; y = y_hi * 2 + y_lo), z: 8, core: 2. Of those that a mesh axis runs over, the one named last changes fastest.
Arguments:
- history: bfloat16 [8192, 1024], P('ctx', 'cand'), may hold values from -6 to 6
- head_weights: bfloat16 [1024, 4096], P(None, 'cand'), may hold values from -0.1875 to 0.1875
- merge_weights: bfloat16 [1024, 1024], P('cand'), may hold values from -0.1875 to 0.1875
- cand_table: bfloat16 [4096, 1024], P('cand'), may hold values from -6 to 6
- user_weights: bfloat16 [1024, 512], P('cand'), may hold values from -0.1875 to 0.1875
- item_weights: bfloat16 [1024, 512], replicated, may hold values from -0.1875 to 0.1875
- score_weights: float32 [512], replicated, may hold values from -0.4 to 0.4
- request_points: int32 [256], replicated, may hold values from 0 to 8191, as said below
- candidate_owner: int32 [256, 512], P('ctx'), may hold values from 0 to 7
- candidate_row: int32 [256, 512], P('ctx'), may hold values from 0 to 511
- relevance: int32 [256, 512], P('ctx'), may hold values from 0 to 3
Outputs:
- losses: float32 [256], P('ctx')
- history_grad: float32 [8192, 1024], P('ctx', 'cand')
- grad_heads: float32 [1024, 4096], P('ctx', 'cand')
- grad_merge: float32 [1024, 1024], P('cand', 'ctx')
Inputs may be any that keep to these rules, and one draw needn't show every extreme that they name: `request_points`: the last request is made at the last position of the history.
All inputs are finite; a program needn't handle non-finite values.
Results may differ from a plain program's by a relative error of at most 0.012.
The roundings to bfloat16 on the way count: a program that leaves them out, or rounds other values in their place, can miss the bound.
Values may be sent and summed in bfloat16 or wider, within the bound.
No kernel may reach another device: no remote copies, remote signals or barrier semaphores. Data moves between devices by JAX's collectives and lax.ppermute only.
A program may use at most 64 MiB of HBM per device.

v0:
```python
import jax
import jax.numpy as jnp
from jax import lax
from jax.sharding import PartitionSpec as P

HEAD = 128


norm_eps = 1e-05


def silu_slope(argument):
    sigmoid_part = jax.nn.sigmoid(argument)
    return sigmoid_part * (1.0 + argument * (1.0 - sigmoid_part))


def layer_norm(argument):
    centred = argument - jnp.mean(argument, -1, keepdims=True)
    inverse = lax.rsqrt(jnp.mean(centred * centred, -1, keepdims=True) + norm_eps)
    return (centred * inverse, inverse)


def norm_back(gradient, normed, inverse):
    return inverse * (
        gradient
        - jnp.mean(gradient, -1, keepdims=True)
        - normed * jnp.mean(gradient * normed, -1, keepdims=True)
    )


def place_scores(queries, key_heads, query_place, key_start):
    scaling = queries.shape[-1] ** (-0.5)
    logits = (
        jnp.einsum("qhd,khd->hqk", queries, key_heads, preferred_element_type=jnp.float32) * scaling
    )
    key_place = key_start + jnp.arange(key_heads.shape[0], dtype=jnp.int32)
    allowed = (key_place[None, :] <= query_place[:, None])[None]
    divisor = (query_place + 1).astype(jnp.float32)[None, :, None]
    return (logits, allowed, divisor)


def tile_scores(queries, key_heads, query_start, key_start):
    query_place = query_start + jnp.arange(queries.shape[0], dtype=jnp.int32)
    return place_scores(queries, key_heads, query_place, key_start)


def per_device(
    history,
    head_weights,
    merge_weights,
    cand_table,
    user_weights,
    item_weights,
    score_weights,
    request_points,
    candidate_owner,
    candidate_row,
    relevance,
):
    row_count = history.shape[0]
    slice_width = history.shape[1]
    first_row = lax.axis_index("ctx") * row_count
    cand_index = lax.axis_index("cand")
    features = lax.all_gather(history, "cand", axis=1, tiled=True)
    x_wide = features.astype(jnp.float32)
    x_normed, x_inverse = layer_norm(x_wide)
    x_low = x_normed.astype(jnp.bfloat16)
    before = jnp.dot(x_low, head_weights, preferred_element_type=jnp.float32)
    project = jax.nn.silu(before).astype(jnp.bfloat16)
    head_count = merge_weights.shape[0] // HEAD
    sections = project.reshape(row_count, head_count, 4, HEAD)
    gate_part = sections[:, :, 0]
    values = sections[:, :, 1]
    queries = sections[:, :, 2]
    key_heads = sections[:, :, 3]
    zero_heads = jnp.zeros((row_count, head_count, HEAD), jnp.float32)
    last_row = first_row + row_count - 1
    scaling = HEAD ** (-0.5)
    all_keys, all_values = (
        lax.all_gather(key_heads, "ctx", axis=0, tiled=True),
        lax.all_gather(values, "ctx", axis=0, tiled=True),
    )

    def forward_compute(current):
        logits, allowed, divisor = tile_scores(queries, all_keys, first_row, 0)
        weight = jnp.where(allowed, jax.nn.silu(logits) / divisor, 0.0).astype(jnp.bfloat16)
        return jnp.einsum("hqk,khd->qhd", weight, all_values, preferred_element_type=jnp.float32)

    attended = lax.cond(0 <= last_row, forward_compute, lambda current: current, zero_heads)
    normed, inverse = layer_norm(attended)
    gated = (
        (normed * gate_part.astype(jnp.float32))
        .astype(jnp.bfloat16)
        .reshape(row_count, head_count * HEAD)
    )
    head_total = lax.psum_scatter(
        jnp.dot(gated, merge_weights, preferred_element_type=jnp.float32),
        "cand",
        scatter_dimension=1,
        tiled=True,
    )
    layer_out = (history.astype(jnp.float32) + head_total).astype(jnp.bfloat16)
    positions = first_row + jnp.arange(row_count, dtype=jnp.int32)
    matches = (request_points[:, None] == positions[None, :]).astype(jnp.bfloat16)
    own_rows = lax.psum_scatter(
        jnp.dot(matches, layer_out, preferred_element_type=jnp.float32),
        "ctx",
        scatter_dimension=0,
        tiled=True,
    )
    user_part = jnp.dot(
        own_rows.astype(jnp.bfloat16), user_weights, preferred_element_type=jnp.float32
    )
    user_proj = lax.psum(user_part, "cand")
    item_proj = jnp.dot(cand_table, item_weights, preferred_element_type=jnp.float32)
    owned = candidate_owner == cand_index
    pre_score = user_proj[:, None, :] + item_proj[candidate_row]
    score_part = jnp.where(owned, jnp.sum(jax.nn.silu(pre_score) * score_weights, -1), 0.0)
    scores = lax.psum(score_part, "cand")
    log_total = jnp.log(jnp.sum(jnp.exp(scores), -1, keepdims=True))
    target = (relevance + 1).astype(jnp.float32)
    target = target / jnp.sum(target, -1, keepdims=True)
    losses = log_total[:, 0] - jnp.sum(target * scores, -1)
    d_score = jnp.exp(scores - log_total) - target
    d_pre = jnp.where(
        owned[:, :, None], d_score[:, :, None] * score_weights * silu_slope(pre_score), 0.0
    )
    d_user = lax.psum(jnp.sum(d_pre, 1), "cand")
    d_picked = jnp.dot(d_user, user_weights.astype(jnp.float32).T, precision=lax.Precision.HIGHEST)
    all_grads = lax.all_gather(d_picked, "ctx", axis=0, tiled=True)
    matches_all = (request_points[:, None] == positions[None, :]).astype(jnp.float32)
    d_layer = lax.dot_general(
        matches_all, all_grads, (((0,), (0,)), ((), ())), precision=lax.Precision.HIGHEST
    )
    d_full = lax.all_gather(d_layer, "cand", axis=1, tiled=True)
    d_gated = jnp.dot(d_full, merge_weights.astype(jnp.float32).T, precision=lax.Precision.HIGHEST)
    d_gated = d_gated.reshape(row_count, head_count, HEAD)
    d_gate = d_gated * normed
    d_attended = norm_back(d_gated * gate_part.astype(jnp.float32), normed, inverse).astype(
        jnp.bfloat16
    )
    merge_term = lax.dot_general(
        gated.astype(jnp.float32), d_full, (((0,), (0,)), ((), ())), precision=lax.Precision.HIGHEST
    )
    grad_merge = lax.psum_scatter(merge_term, "ctx", scatter_dimension=1, tiled=True)

    def query_compute(current):
        logits, allowed, divisor = tile_scores(queries, all_keys, first_row, 0)
        slopes = jnp.einsum(
            "qhd,khd->hqk", d_attended, all_values, preferred_element_type=jnp.float32
        )
        d_logit = jnp.where(allowed, slopes * silu_slope(logits) / divisor, 0.0).astype(
            jnp.bfloat16
        )
        return (
            jnp.einsum("hqk,khd->qhd", d_logit, all_keys, preferred_element_type=jnp.float32)
            * scaling
        )

    d_query = lax.cond(0 <= last_row, query_compute, lambda current: current, zero_heads)
    begin = jnp.int32(0)
    piece_queries = lax.all_gather(queries, "ctx", axis=0, tiled=True)
    piece_grads = lax.all_gather(d_attended, "ctx", axis=0, tiled=True)
    piece_rows = piece_queries.shape[0]

    def key_compute(current):
        logits, allowed, divisor = tile_scores(piece_queries, key_heads, begin, first_row)
        weight = jnp.where(allowed, jax.nn.silu(logits) / divisor, 0.0).astype(jnp.bfloat16)
        slopes = jnp.einsum("qhd,khd->hqk", piece_grads, values, preferred_element_type=jnp.float32)
        d_logit = jnp.where(allowed, slopes * silu_slope(logits) / divisor, 0.0).astype(
            jnp.bfloat16
        )
        key_grad = (
            jnp.einsum("hqk,qhd->khd", d_logit, piece_queries, preferred_element_type=jnp.float32)
            * scaling
        )
        value_grad = jnp.einsum(
            "hqk,qhd->khd", weight, piece_grads, preferred_element_type=jnp.float32
        )
        return (key_grad, value_grad)

    d_key, d_value = lax.cond(
        begin + piece_rows - 1 >= first_row,
        key_compute,
        lambda current: current,
        (zero_heads, zero_heads),
    )
    d_project = jnp.stack([d_gate, d_value, d_query, d_key], 2).reshape(
        row_count, head_count * 4 * HEAD
    )
    d_before = (d_project * silu_slope(before)).astype(jnp.bfloat16)
    grad_heads = lax.psum_scatter(
        lax.dot_general(
            x_low, d_before, (((0,), (0,)), ((), ())), preferred_element_type=jnp.float32
        ),
        "ctx",
        scatter_dimension=0,
        tiled=True,
    )
    normed_part = jnp.dot(d_before, head_weights.T, preferred_element_type=jnp.float32)
    column_start = cand_index * slice_width
    d_normed = lax.psum(normed_part, "cand")
    d_input = lax.dynamic_slice_in_dim(
        norm_back(d_normed, x_normed, x_inverse), column_start, slice_width, 1
    )
    history_grad = d_layer + d_input
    return (losses, history_grad, grad_heads, grad_merge)


def solution(mesh):
    return jax.shard_map(
        per_device,
        mesh=mesh,
        in_specs=(
            P("ctx", "cand"),
            P(None, "cand"),
            P("cand", None),
            P("cand", None),
            P("cand", None),
            P(),
            P(),
            P(),
            P("ctx", None),
            P("ctx", None),
            P("ctx", None),
        ),
        out_specs=(P("ctx"), P("ctx", "cand"), P("ctx", "cand"), P("cand", "ctx")),
        check_vma=False,
    )
```

profile of v0, /device:TPU:32, one launch (start us, length us, event | category | flops | bytes accessed | tf_op | source)
XLA Modules:
  0.0 2184.5 jit_solution(12242069571843602109)
XLA Ops:
  7.2 17.2 all_gather.21
  24.7 2.3 multiply_convert_fusion.1
  30.1 302.3 %all-gather.11.cloned.1.call-done = bf16[8192,1,1,128]{3,0,2,1:T(8,128)(2,1)} async-done(((bf16[128,1,1,128]{3,0,2,1:T(8,128)(2,1)}), bf16[8192,1,1,128]{3,0,2,1:T(8,128)(2,1)}) %all-gather.11.cloned.1.call-update) | async-done | bytes 2097168 | tf_op jit(solution)/shard_map/all_gather | solution.py:80
  332.4 301.4 %all-gather.13.cloned.1.call-done = bf16[8192,1,1,128]{3,0,2,1:T(8,128)(2,1)} async-done(((bf16[128,1,1,128]{3,0,2,1:T(8,128)(2,1)}), bf16[8192,1,1,128]{3,0,2,1:T(8,128)(2,1)}) %all-gather.13.cloned.1.call-update) | async-done | bytes 2097168 | tf_op jit(solution)/shard_map/all_gather | solution.py:81
  633.9 4.4 conditional.3
  633.9 4.4 fusion.98
  638.4 1.1 fusion.105
  640.9 1.3 dynamic-slice
  642.8 1.9 fusion.106
  644.8 8.9 gather_fusion
  653.7 20.1 reduce-scatter.4.cloned.1.call-done
  673.8 1.1 fusion.70
  674.8 310.1 %all-reduce.5 = bf16[256,128]{1,0:T(8,128)(2,1)S(1)} all-reduce(f32[256,128]{1,0:T(8,128)S(1)} %fusion.70), channel_id=6, replica_groups=mesh['ctx'=64,'cand'=8] {'ctx'}, use_global_device_ids=true, to_apply=%region_7.8.clone | all-reduce | flops 32768 | bytes 196608
  985.1 14.4 psum.28
  999.6 3.6 multiply_reduce_fusion
  1003.2 1.5 broadcast_select_fusion
  1004.6 15.2 psum.29
  1019.8 0.9 exponential_reduce_fusion
  1022.0 3.6 select_reduce_fusion
  1025.6 14.5 psum.30
  1040.0 1.1 convolution_bitcast_fusion
  1041.1 150.8 %all-gather.3 = f32[64,4,128]{2,1,0:T(4,128)S(1)} all-gather(f32[1,4,128]{2,1,0:T(4,128)S(1)} %convolution_bitcast_fusion), channel_id=1, replica_groups=mesh['ctx'=64,'cand'=8] {'ctx'}, dimensions={0}, use_global_device_ids=true | all-gather | bytes 133120 | tf_op jit(solution)/shard_map/all_gather | solution.py:130
  1191.9 1.0 fusion.68
  1193.6 14.9 all_gather.25
  1208.5 0.8 copy-done.2
  1209.3 1.4 fusion.82
  1210.7 1.3 fusion.85
  1212.3 0.8 copy.63
  1213.1 1.5 copy.64
  1214.6 10.4 conditional.5
  1214.6 3.4 convolution_multiply_fusion.3
  1218.0 6.1 fusion.55
  1224.1 0.9 copy.54
  1225.0 218.3 %all-gather.9.cloned.1.call-done = bf16[8192,1,128]{0,2,1:T(8,128)(2,1)} async-done(((bf16[128,1,128]{0,2,1:T(8,128)(2,1)}), bf16[8192,1,128]{0,2,1:T(8,128)(2,1)}) %all-gather.9.cloned.1.call-update) | async-done | bytes 2097168 | tf_op jit(solution)/shard_map/all_gather | solution.py:163
  1443.3 15.6 conditional.4
  1443.3 4.4 convolution_multiply_fusion.1
  1447.7 6.3 fusion.29
  1454.8 4.1 fusion.21
  1459.0 1.0 pad_maximum_fusion
  1460.1 1.1 multiply_convert_fusion
  1461.1 2.5 fusion.107
  1463.7 1.4 fusion.108
  1465.2 1.9 fusion.72
  1467.1 70.5 %all-reduce.4.cloned.1.call-done = f32[128,1024]{1,0:T(8,128)} async-done(((f32[128,1024]{1,0:T(8,128)}), f32[128,1024]{1,0:T(8,128)}) %all-reduce.4.cloned.1.call-update) | async-done | bytes 524304 | tf_op jit(solution)/shard_map/psum | solution.py:202
  1537.6 1.3 fusion.97
  1538.9 1.6 fusion.81
  1540.5 319.6 %reduce-scatter.8.cloned.1.call-done = f32[128,16]{0,1:T(8,128)} async-done(((f32[128,1024]{0,1:T(8,128)}), f32[128,16]{0,1:T(8,128)}) %reduce-scatter.8.cloned.1.call-update) | async-done | bytes 8208 | tf_op jit(solution)/shard_map/reduce_scatter | solution.py:145
  1860.1 317.5 %reduce-scatter.6.cloned.1.call-done = f32[16,512]{1,0:T(8,128)} async-done(((f32[1024,512]{1,0:T(8,128)}), f32[16,512]{1,0:T(8,128)}) %reduce-scatter.6.cloned.1.call-update) | async-done | bytes 32784 | tf_op jit(solution)/shard_map/reduce_scatter | solution.py:192
  (99 shorter events, 8.3 us)
Async XLA Ops:
  7.2 635.7 %copy-start = (bf16[512,1024]{1,0:T(8,128)(2,1)S(1)}, bf16[512,1024]{1,0:T(8,128)(2,1)}, u32[]{:S(2)}) copy-start(bf16[512,1024]{1,0:T(8,128)(2,1)} %param.20) | copy-start | bytes 3145732
  7.2 325.2 %all-gather.11.cloned.1.call-start = ((), (), s32[]{:S(2)}) async-start(), calls=%async_computation.8 | async-start | bytes 2129920 | tf_op jit(solution)/shard_map/all_gather | solution.py:80
  24.5 2.6 copy-start.20
  24.7 2.3 copy-start.18
  27.3 0.6 copy-start.9
  27.3 606.5 %copy-start.8 = (bf16[128,1,1,128]{3,2,0,1:T(2,128)(2,1)}, bf16[128,1,1,128]{3,2,0,1:T(2,128)(2,1)S(1)}, u32[]{:S(2)}) copy-start(bf16[128,1,1,128]{3,2,0,1:T(2,128)(2,1)S(1)} %get-tuple-element.110) | copy-start | bytes 98308
  28.6 605.3 %all-gather.13.cloned.1.call-start = ((), (), s32[]{:S(2)}) async-start(), calls=%async_computation.9 | async-start | bytes 2129920 | tf_op jit(solution)/shard_map/all_gather | solution.py:81
  29.3 644.4 %reduce-scatter.4.cloned.1.call-start = ((), (), s32[]{:S(2)}) async-start(), calls=%async_computation.3 | async-start | bytes 589824 | tf_op jit(solution)/shard_map/reduce_scatter | solution.py:96
  633.8 4.5 copy-start.5
  633.8 6.4 copy-start.17
  633.8 6.5 copy-start.14
  638.3 1.9 copy-start.16
  638.4 1.9 copy-start.22
  639.5 585.6 %all-gather.15.cloned.1.call-start = ((), (), s32[]{:S(2)}) async-start(), calls=%async_computation.10 | async-start | bytes 2129920 | tf_op jit(solution)/shard_map/all_gather | solution.py:162
  640.2 803.2 %all-gather.9.cloned.1.call-start = ((), (), s32[]{:S(2)}) async-start(), calls=%async_computation.4 | async-start | bytes 2129920 | tf_op jit(solution)/shard_map/all_gather | solution.py:163
  640.2 33.5 %copy-start.24 = (s32[128]{0:T(128)}, s32[128]{0:T(128)S(1)}, u32[]{:S(2)}) copy-start(s32[128]{0:T(128)S(1)} %iota_add_fusion.3) | copy-start | bytes 1540
  644.8 29.0 %copy-start.12 = (bf16[128,128]{1,0:T(8,128)(2,1)S(1)}, bf16[128,128]{1,0:T(8,128)(2,1)}, u32[]{:S(2)}) copy-start(bf16[128,128]{1,0:T(8,128)(2,1)} %param.17) | copy-start | bytes 98308
  644.8 29.0 %copy-start.23 = (s32[256]{0:T(256)S(1)}, s32[256]{0:T(256)}, u32[]{:S(2)}) copy-start(s32[256]{0:T(256)} %param.24) | copy-start | bytes 3076
  644.8 340.2 %copy-start.10 = (bf16[128,512]{1,0:T(8,128)(2,1)S(1)}, bf16[128,512]{1,0:T(8,128)(2,1)}, u32[]{:S(2)}) copy-start(bf16[128,512]{1,0:T(8,128)(2,1)} %param.21) | copy-start | bytes 393220
  644.8 354.7 %copy-start.15 = (f32[512]{0:T(512)S(1)}, f32[512]{0:T(512)}, u32[]{:S(2)}) copy-start(f32[512]{0:T(512)} %param.23) | copy-start | bytes 6148
  1003.2 211.4 %copy-start.4 = (bf16[8192,1,1,128]{3,0,2,1:T(8,128)(2,1)S(1)}, bf16[8192,1,1,128]{3,0,2,1:T(8,128)(2,1)}, u32[]{:S(2)}) copy-start(bf16[8192,1,1,128]{3,0,2,1:T(8,128)(2,1)} %all-gather.11.cloned.1.call-done) | copy-start | bytes 6291460
  1192.9 0.6 copy-start.6
  1208.5 0.8 copy-start.2
  1212.0 325.6 %all-reduce.4.cloned.1.call-start = ((), (), s32[]{:S(2)}) async-start(), calls=%async_computation.5 | async-start | bytes 1048576 | tf_op jit(solution)/shard_map/psum | solution.py:202
  1214.6 3.4 copy-start.13
  1225.0 218.3 %copy-start.11 = (f32[128,1,1,128]{0,3,2,1:T(8,128)}, f32[128,1,1,128]{0,3,2,1:T(8,128)S(1)}, u32[]{:S(2)}) copy-start(f32[128,1,1,128]{0,3,2,1:T(8,128)S(1)} %get-tuple-element.94) | copy-start | bytes 196612
  1443.3 4.4 copy-start.1
  1458.9 4.8 copy-start.3
  1459.0 6.2 copy-start.19
  1459.0 6.2 copy-start.21
  1463.7 75.2 %copy-start.7 = (f32[128,128]{1,0:T(8,128)S(1)}, f32[128,128]{1,0:T(8,128)}, u32[]{:S(2)}) copy-start(f32[128,128]{1,0:T(8,128)} %copy-done.6) | copy-start | bytes 196612
  1463.7 396.4 %reduce-scatter.8.cloned.1.call-start = ((), (), s32[]{:S(2)}) async-start(), calls=%async_computation.7 | async-start | bytes 532480 | tf_op jit(solution)/shard_map/reduce_scatter | solution.py:145
  1465.1 712.5 %reduce-scatter.6.cloned.1.call-start = ((), (), s32[]{:S(2)}) async-start(), calls=%async_computation.6 | async-start | bytes 2129920 | tf_op jit(solution)/shard_map/reduce_scatter | solution.py:192
Sparse Core Ops, SparseCore 0:
  28.7 303.6 all-gather.10
  334.5 299.3 all-gather.12
  639.6 34.1 reduce-scatter.3
  675.9 303.8 all-gather.14
  1212.2 231.1 all-gather.8
  1463.8 73.7 all-reduce.3
  1541.0 319.1 reduce-scatter.7
  1863.7 313.8 reduce-scatter.5
where the time goes:
time: 2190 us; the launch traced here: 2180 us
  waiting for transfers between devices  1550 us (71%)
  blocking collectives  537 us (25%)
  matrix products  44.4 us (2%)
    reduce_scatter x1, waiting for transfers between devices, per_device(): lax.psum_scatter(merge_term, 'ctx', scatter_dimension=1, tiled=True)  320 us
    reduce_scatter x1, waiting for transfers between devices, per_device(): lax.psum_scatter(lax.dot_general(x_low, d_before, (((0,), (0,)), ((), ())...  318 us
    unnamed x1, blocking collectives  310 us
    all_gather x1, waiting for transfers between devices, per_device(): lax.all_gather(key_heads, 'ctx', axis=0, tiled=True)  302 us
    all_gather x1, waiting for transfers between devices, per_device(): lax.all_gather(values, 'ctx', axis=0, tiled=True)  301 us
    all_gather x1, waiting for transfers between devices, per_device(): piece_grads = lax.all_gather(d_attended, 'ctx', axis=0, tiled=True)  218 us
    all_gather x1, blocking collectives, per_device(): all_grads = lax.all_gather(d_picked, 'ctx', axis=0, tiled=True)  151 us
    psum x1, waiting for transfers between devices, per_device(): d_normed = lax.psum(normed_part, 'cand')  70.5 us
  transfers between devices with their start and end apart: 8, of which 7 were waited for; matrix products, arithmetic and copies ran while one was open for 2% of the time, Pallas kernels for 0%

commit v1 on v0

v1 whole, which is shorter than its diff:
```python
import jax
import jax.numpy as jnp
from jax import lax
from jax.sharding import PartitionSpec as P

HEAD = 128
norm_eps = 1e-05
F32 = jnp.float32
BF16 = jnp.bfloat16


def sigmoid_slope(argument):
    part = jax.nn.sigmoid(argument)
    return argument * part, part * (1.0 + argument * (1.0 - part))


def layer_norm(argument):
    centred = argument - jnp.mean(argument, -1, keepdims=True)
    inverse = lax.rsqrt(jnp.mean(centred * centred, -1, keepdims=True) + norm_eps)
    return (centred * inverse, inverse)


def norm_back(gradient, normed, inverse):
    return inverse * (
        gradient
        - jnp.mean(gradient, -1, keepdims=True)
        - normed * jnp.mean(gradient * normed, -1, keepdims=True)
    )


def mm(left, right, dims=((1,), (0,))):
    return lax.dot_general(left, right, (dims, ((), ())), preferred_element_type=F32)


def mm_split(left, right, dims=((1,), (0,))):
    high = left.astype(BF16)
    rest = left - high.astype(F32)
    middle = rest.astype(BF16)
    low = (rest - middle.astype(F32)).astype(BF16)
    count = left.shape[0]
    product = mm(jnp.concatenate([high, middle, low], 0), right, dims)
    return product[:count] + product[count : 2 * count] + product[2 * count :]


def swap(block, axis):
    return lax.all_to_all(block, axis, 0, 0, tiled=True)


def send_all(block, axis, size):
    return swap(jnp.broadcast_to(block[None], (size,) + block.shape), axis)


def per_device(
    n_ctx,
    n_cand,
    history,
    head_weights,
    merge_weights,
    cand_table,
    user_weights,
    item_weights,
    score_weights,
    request_points,
    candidate_owner,
    candidate_row,
    relevance,
):
    rows, width = history.shape
    requests = request_points.shape[0]
    own = requests // n_ctx
    features = width * n_cand
    hidden = user_weights.shape[1]
    table_rows = cand_table.shape[0]
    strip = features // n_ctx
    ctx = lax.axis_index("ctx")
    cand = lax.axis_index("cand")
    first_row = ctx * rows
    scaling = HEAD ** (-0.5)

    item_proj = mm(cand_table, item_weights).astype(BF16)
    packed = jnp.concatenate(
        [merge_weights[:, :hidden], merge_weights[:, hidden:], user_weights, item_proj], 0
    )
    pack_rows = packed.shape[0]
    table = lax.all_gather(packed, "cand", axis=0, tiled=True)

    positions = first_row + jnp.arange(rows, dtype=jnp.int32)
    matches = (request_points[:, None] == positions[None, :]).astype(BF16)
    picked = mm(matches, history).astype(BF16).reshape(n_ctx, own, width)
    picked = swap(picked, "ctx")
    picked = jnp.sum(picked.astype(F32), 0).astype(BF16)

    pad = jnp.zeros((8 - own, width), BF16)
    both = lax.all_gather(
        jnp.concatenate([history, picked, pad], 0), "cand", axis=1, tiled=True
    )
    x_wide = both.astype(F32)
    x_normed, x_inverse = layer_norm(x_wide)
    x_low = x_normed.astype(BF16)
    before = mm(x_low, head_weights)
    smooth, slope = sigmoid_slope(before)
    project = smooth.astype(BF16)
    values = project[:rows, HEAD : 2 * HEAD]
    key_heads = project[:rows, 3 * HEAD :]
    gate = project[rows : rows + own, :HEAD].astype(F32)
    own_queries = project[rows : rows + own, 2 * HEAD : 3 * HEAD]
    request_low = x_low[rows : rows + own]

    queries = send_all(own_queries, "ctx", n_ctx).reshape(requests, HEAD)
    logits = mm(queries, key_heads, ((1,), (1,))) * scaling
    allowed = positions[None, :] <= request_points[:, None]
    divisor = (request_points + 1).astype(F32)[:, None]
    logit_smooth, logit_slope = sigmoid_slope(logits)
    weight = jnp.where(allowed, logit_smooth / divisor, 0.0).astype(BF16)
    attended = swap(mm(weight, values).reshape(n_ctx, own, HEAD), "ctx")
    attended = jnp.sum(attended, 0)
    normed, inverse = layer_norm(attended)
    gated = (normed * gate).astype(BF16)

    gated_full = send_all(gated, "cand", n_cand)
    gated_full = gated_full.transpose(1, 0, 2).reshape(own, features)
    blocks = table.reshape(n_cand, pack_rows, hidden)
    merge_left = blocks[:, :HEAD].reshape(features, hidden)
    merge_right = blocks[:, HEAD : 2 * HEAD].reshape(features, hidden)
    user_full = blocks[:, 2 * HEAD : 2 * HEAD + width].reshape(features, hidden)
    merged = jnp.concatenate([mm(gated_full, merge_left), mm(gated_full, merge_right)], 1)
    layer_out = (x_wide[rows : rows + own] + merged).astype(BF16)
    user_proj = mm(layer_out, user_full)

    place = candidate_owner * pack_rows + (pack_rows - table_rows) + candidate_row
    items = table[place].astype(F32)
    pre_score = user_proj[:, None, :] + items
    pre_smooth, pre_slope = sigmoid_slope(pre_score)
    scores = jnp.sum(pre_smooth * score_weights, -1)
    log_total = jnp.log(jnp.sum(jnp.exp(scores), -1, keepdims=True))
    target = (relevance + 1).astype(F32)
    target = target / jnp.sum(target, -1, keepdims=True)
    losses = log_total[:, 0] - jnp.sum(target * scores, -1)
    d_score = jnp.exp(scores - log_total) - target
    d_user = jnp.sum(d_score[:, :, None] * pre_slope, 1) * score_weights
    d_picked = mm_split(d_user, user_full, ((1,), (1,)))
    d_gated = mm_split(d_picked, merge_weights, ((1,), (1,)))
    d_attended = norm_back(d_gated * gate, normed, inverse).astype(BF16)
    d_before_gate = (d_gated * normed * slope[rows : rows + own, :HEAD]).astype(BF16)

    strips = jnp.concatenate(
        [
            request_low.reshape(own, n_ctx, strip),
            d_picked.astype(BF16).reshape(own, n_ctx, strip),
        ],
        2,
    ).transpose(1, 0, 2)
    strips = jnp.pad(strips, ((0, 0), (0, 0), (0, HEAD - 2 * strip)))
    shared = jnp.concatenate([d_attended, gated, d_before_gate], 0)
    sent = jnp.concatenate(
        [jnp.broadcast_to(shared[None], (n_ctx,) + shared.shape), strips], 1
    )
    sent = swap(sent, "ctx")
    all_grads = sent[:, :own].reshape(requests, HEAD)
    all_gated = sent[:, own : 2 * own].reshape(requests, HEAD)
    all_gate_grads = sent[:, 2 * own : 3 * own].reshape(requests, HEAD)
    all_strips = sent[:, 3 * own :].reshape(requests, HEAD)
    x_strip = all_strips[:, :strip]
    d_strip = all_strips[:, strip : 2 * strip]
    grad_merge = mm(all_gated, d_strip, ((0,), (0,)))
    slopes = mm(all_grads, values, ((1,), (1,)))
    d_logit = jnp.where(allowed, slopes * logit_slope / divisor, 0.0).astype(BF16)
    d_query = (mm(d_logit, key_heads) * scaling).astype(BF16)
    d_key = mm(d_logit, queries, ((0,), (0,))) * scaling
    d_value = mm(weight, all_grads, ((0,), (0,)))
    d_value = (d_value * slope[:rows, HEAD : 2 * HEAD]).astype(BF16)
    d_key = (d_key * slope[:rows, 3 * HEAD :]).astype(BF16)
    dense = jnp.concatenate([d_value, d_key], 1)
    dense_grad = mm(x_low[:rows], dense, ((0,), (0,))).astype(BF16)
    dense_grad = dense_grad.reshape(n_ctx, strip, 2 * HEAD)
    dense_grad = jnp.concatenate(
        [dense_grad[:, :, :HEAD], dense_grad[:, :, HEAD:], d_query.reshape(n_ctx, own, HEAD)], 1
    )
    dense_grad = jnp.sum(swap(dense_grad, "ctx").astype(F32), 0)
    own_query_grad = dense_grad[2 * strip :]
    d_before_query = (own_query_grad * slope[rows : rows + own, 2 * HEAD : 3 * HEAD]).astype(BF16)

    weights_dense = jnp.concatenate(
        [head_weights[:, HEAD : 2 * HEAD], head_weights[:, 3 * HEAD :]], 1
    )
    weights_request = jnp.concatenate(
        [head_weights[:, :HEAD], head_weights[:, 2 * HEAD : 3 * HEAD]], 1
    )
    request_before = jnp.concatenate([d_before_gate, d_before_query], 1)
    back_dense = norm_back(
        mm(dense, weights_dense, ((1,), (1,))), x_normed[:rows], x_inverse[:rows]
    )
    back_request = norm_back(
        mm(request_before, weights_request, ((1,), (1,))),
        x_normed[rows : rows + own],
        x_inverse[rows : rows + own],
    )
    back = jnp.concatenate(
        [back_dense, back_request, jnp.zeros((8 - own, features), F32)], 0
    ).astype(BF16)
    back = back.reshape(rows + 8, n_cand, width).transpose(1, 0, 2)
    back = jnp.sum(swap(back, "cand").astype(F32), 0)
    own_slice = lax.dynamic_slice_in_dim(d_picked, cand * width, width, 1)
    request_grad = back[rows : rows + own] + own_slice
    final = jnp.concatenate([request_grad.astype(BF16), d_before_query], 0)
    final = send_all(final, "ctx", n_ctx)
    all_request_grad = final[:, :own].reshape(requests, width)
    all_query_grads = final[:, own:].reshape(requests, HEAD)
    history_grad = back[:rows] + mm(matches, all_request_grad, ((0,), (0,)))
    gate_query = mm(
        x_strip, jnp.concatenate([all_gate_grads, all_query_grads], 1), ((0,), (0,))
    )
    grad_heads = jnp.concatenate(
        [
            gate_query[:, :HEAD],
            dense_grad[:strip],
            gate_query[:, HEAD:],
            dense_grad[strip : 2 * strip],
        ],
        1,
    )
    return (losses, history_grad, grad_heads, grad_merge)


def solution(mesh):
    n_ctx = mesh.shape["ctx"]
    n_cand = mesh.shape["cand"]

    def body(*args):
        return per_device(n_ctx, n_cand, *args)

    return jax.shard_map(
        body,
        mesh=mesh,
        in_specs=(
            P("ctx", "cand"),
            P(None, "cand"),
            P("cand", None),
            P("cand", None),
            P("cand", None),
            P(),
            P(),
            P(),
            P("ctx", None),
            P("ctx", None),
            P("ctx", None),
        ),
        out_specs=(P("ctx"), P("ctx", "cand"), P("ctx", "cand"), P("cand", "ctx")),
        check_vma=False,
    )
```

time: 2190 us -> 249 us (0.11)
  the two profiles are of different devices: /device:TPU:32 before, /device:TPU:8 now
where the time goes in v1:
time: 249 us; the launch traced here: 248 us
  waiting for transfers between devices  82.9 us (33%)
  starting transfers between devices  55.8 us (22%)
  blocking collectives  37.7 us (15%)
  local copies, waits for them, and re-layouts  19.8 us (8%)
  other arithmetic  19 us (8%)
  matrix products  18.1 us (7%)
  between operations  14.6 us (6%)
    all_to_all x7, waiting for transfers between devices, swap(): return lax.all_to_all(block, axis, 0, 0, tiled=True)  82.9 us
    all_to_all x7, starting transfers between devices, swap(): return lax.all_to_all(block, axis, 0, 0, tiled=True)  55.7 us
    all_gather x1, blocking collectives, per_device(): lax.all_gather(jnp.concatenate([history, picked, pad], 0), 'cand', axis=1...  20.4 us
    dot_general x20, matrix products, mm(): lax.dot_general(left, right, (dims, ((), ())), preferred_element_type=F32)  18.1 us
    all_to_all x1, blocking collectives, swap(): return lax.all_to_all(block, axis, 0, 0, tiled=True)  17.3 us
    gather x1, local copies, waits for them, and re-layouts, per_device(): items = table[place].astype(F32)  12.6 us
  transfers between devices with their start and end apart: 8, of which 7 were waited for; matrix products, arithmetic and copies ran while one was open for 5% of the time, Pallas kernels for 0%

profile of v1, /device:TPU:8, one launch (start us, length us, event | category | flops | bytes accessed | tf_op | source)
XLA Modules:
  0.0 247.9 jit_solution(2897141713945313099)
XLA Ops:
  7.2 1.1 fusion.95
  8.5 2.0 convolution_convert_fusion.1
  10.6 1.9 pad_maximum_fusion
  12.5 0.9 convolution_convert_fusion.2
  13.4 14.8 %all-to-all-start = ((bf16[64,4,128]{2,1,0:T(4,128)(2,1)}), bf16[64,4,128]{2,1,0:T(4,128)(2,1)S(1)}, u32[]{:S(2)}, u32[]{:S(2)}) async-start(bf16[64,4,128]{2,1,0:T(4,128)(2,1)} %bitcast), calls=%async_computation | async-start | bytes 131072 | tf_op jit(solution)/shard_map/all_to_all | solution.py:46
  28.3 9.7 %all-to-all-done = bf16[64,4,128]{2,1,0:T(4,128)(2,1)S(1)} async-done(((bf16[64,4,128]{2,1,0:T(4,128)(2,1)}), bf16[64,4,128]{2,1,0:T(4,128)(2,1)S(1)}, u32[]{:S(2)}, u32[]{:S(2)}) %all-to-all-start) | async-done | bytes 65568 | tf_op jit(solution)/shard_map/all_to_all | solution.py:46
  38.2 20.4 %all_gather.6 = bf16[136,1024]{1,0:T(8,128)(2,1)S(1)} all-gather(bf16[136,128]{1,0:T(8,128)(2,1)S(1)} %maximum_maximum_fusion), channel_id=1, replica_groups=mesh['ctx'=64,'cand'=8] {'cand'}, dimensions={1}, use_global_device_ids=true | all-gather | bytes 313344 | tf_op jit(solution)/shard_map/all_gather | solution.py:94
  59.0 1.1 subtract_multiply_fusion
  60.0 1.1 add_multiply_fusion
  61.8 8.4 %all-to-all-start.1 = ((bf16[64,4,128]{2,1,0:T(4,128)(2,1)}), bf16[64,4,128]{2,1,0:T(4,128)(2,1)S(1)}, u32[]{:S(2)}, u32[]{:S(2)}) async-start(bf16[64,4,128]{2,1,0:T(4,128)(2,1)} %broadcast_in_dim.20), calls=%async_computation.1 | async-start | bytes 131072 | tf_op jit(solution)/shard_map/all_to_all | solution.py:46
  70.3 18.2 %all-to-all-done.1 = bf16[64,4,128]{2,1,0:T(4,128)(2,1)S(1)} async-done(((bf16[64,4,128]{2,1,0:T(4,128)(2,1)}), bf16[64,4,128]{2,1,0:T(4,128)(2,1)S(1)}, u32[]{:S(2)}, u32[]{:S(2)}) %all-to-all-start.1) | async-done | bytes 65568 | tf_op jit(solution)/shard_map/all_to_all | solution.py:46
  88.5 0.8 fusion.35
  89.3 0.8 fusion.54
  90.1 10.8 %all-to-all-start.2 = ((f32[64,4,128]{2,1,0:T(4,128)}), f32[64,4,128]{2,1,0:T(4,128)S(1)}, u32[]{:S(2)}, u32[]{:S(2)}) async-start(f32[64,4,128]{2,1,0:T(4,128)} %bitcast.2), calls=%async_computation.2 | async-start | bytes 262144 | tf_op jit(solution)/shard_map/all_to_all | solution.py:46
  101.6 9.8 %all-to-all-done.2 = f32[64,4,128]{2,1,0:T(4,128)S(1)} async-done(((f32[64,4,128]{2,1,0:T(4,128)}), f32[64,4,128]{2,1,0:T(4,128)S(1)}, u32[]{:S(2)}, u32[]{:S(2)}) %all-to-all-start.2) | async-done | bytes 131104 | tf_op jit(solution)/shard_map/all_to_all | solution.py:46
  112.5 6.9 %all-to-all-start.3 = ((bf16[8,4,128]{2,1,0:T(4,128)(2,1)}), bf16[8,4,128]{2,1,0:T(4,128)(2,1)S(1)}, u32[]{:S(2)}, u32[]{:S(2)}) async-start(bf16[8,4,128]{2,1,0:T(4,128)(2,1)} %broadcast_in_dim.22), calls=%async_computation.3 | async-start | bytes 16384 | tf_op jit(solution)/shard_map/all_to_all | solution.py:46
  119.4 0.7 convert_reduce_fusion.3
  120.2 0.7 reshape.151
  120.9 1.3 slice.199
  122.2 4.8 %all-to-all-done.3 = bf16[8,4,128]{2,1,0:T(4,128)(2,1)S(1)} async-done(((bf16[8,4,128]{2,1,0:T(4,128)(2,1)}), bf16[8,4,128]{2,1,0:T(4,128)(2,1)S(1)}, u32[]{:S(2)}, u32[]{:S(2)}) %all-to-all-start.3) | async-done | bytes 8224 | tf_op jit(solution)/shard_map/all_to_all | solution.py:46
  127.1 1.5 convolution_bitcast_fusion.1
  128.5 1.5 convolution_bitcast_fusion
  130.0 0.9 fusion.66
  130.9 12.6 %gather_fusion = bf16[2048,512]{1,0:T(8,128)(2,1)S(1)} fusion(bf16[7168,512]{1,0:T(8,128)(2,1)} %all-gather.2.cloned.1.call-done, s32[2048]{0:T(1024)} %broadcast_clamp_fusion), kind=kCustom, calls=%fused_computation | custom fusion | bytes 4202496 | tf_op jit(solution)/shard_map/gather | solution.py:131
  143.5 2.1 fusion.7
  145.6 0.9 exponential_reduce_fusion
  147.1 0.8 exponential_subtract_fusion
  147.8 2.4 fusion.11
  150.8 1.1 fusion.47
  152.0 0.9 fusion.80
  152.9 0.9 maximum_bitcast_fusion.1
  153.9 0.8 multiply_convert_fusion.4
  155.5 17.3 %all_to_all.40 = bf16[64,16,128]{2,1,0:T(8,128)(2,1)S(1)} all-to-all(bf16[64,16,128]{2,1,0:T(8,128)(2,1)S(1)} %fusion.30), channel_id=1, replica_groups=mesh['ctx'=64,'cand'=8] {'ctx'}, dimensions={0} | all-to-all | bytes 524288 | tf_op jit(solution)/shard_map/all_to_all | solution.py:46
  172.9 1.0 fusion.17
  173.9 1.1 fusion.14
  175.1 1.0 fusion.18
  176.1 0.9 fusion.15
  177.5 0.9 pad_maximum_fusion.1
  178.4 5.5 %all-to-all-start.5 = ((bf16[64,36,128]{2,1,0:T(8,128)(2,1)}), bf16[64,36,128]{2,1,0:T(8,128)(2,1)S(1)}, u32[]{:S(2)}, u32[]{:S(2)}) async-start(bf16[64,36,128]{2,1,0:T(8,128)(2,1)} %pad_maximum_fusion.1), calls=%async_computation.5 | async-start | bytes 1310720 | tf_op jit(solution)/shard_map/all_to_all | solution.py:46
  184.0 1.3 fusion.92
  185.9 17.9 %all-to-all-done.5 = bf16[64,36,128]{2,1,0:T(8,128)(2,1)S(1)} async-done(((bf16[64,36,128]{2,1,0:T(8,128)(2,1)}), bf16[64,36,128]{2,1,0:T(8,128)(2,1)S(1)}, u32[]{:S(2)}, u32[]{:S(2)}) %all-to-all-start.5) | async-done | bytes 589856 | tf_op jit(solution)/shard_map/all_to_all | solution.py:46
  205.2 0.8 maximum_bitcast_fusion
  206.0 3.4 %all-to-all-start.6 = ((bf16[8,136,128]{2,1,0:T(8,128)(2,1)}), bf16[8,136,128]{2,1,0:T(8,128)(2,1)S(1)}, u32[]{:S(2)}, u32[]{:S(2)}) async-start(bf16[8,136,128]{2,1,0:T(8,128)(2,1)} %maximum_bitcast_fusion), calls=%async_computation.6 | async-start | bytes 557056 | tf_op jit(solution)/shard_map/all_to_all | solution.py:46
  209.4 12.9 %all-to-all-done.6 = bf16[8,136,128]{2,1,0:T(8,128)(2,1)S(1)} async-done(((bf16[8,136,128]{2,1,0:T(8,128)(2,1)}), bf16[8,136,128]{2,1,0:T(8,128)(2,1)S(1)}, u32[]{:S(2)}, u32[]{:S(2)}) %all-to-all-start.6) | async-done | bytes 278560 | tf_op jit(solution)/shard_map/all_to_all | solution.py:46
  223.1 5.8 %all-to-all-start.7 = ((bf16[64,8,128]{2,1,0:T(8,128)(2,1)}), bf16[64,8,128]{2,1,0:T(8,128)(2,1)S(1)}, u32[]{:S(2)}, u32[]{:S(2)}) async-start(bf16[64,8,128]{2,1,0:T(8,128)(2,1)} %broadcast_in_dim.26), calls=%async_computation.7 | async-start | bytes 262144 | tf_op jit(solution)/shard_map/all_to_all | solution.py:46
  228.9 0.9 fusion.40
  229.8 9.5 %all-to-all-done.7 = bf16[64,8,128]{2,1,0:T(8,128)(2,1)S(1)} async-done(((bf16[64,8,128]{2,1,0:T(8,128)(2,1)}), bf16[64,8,128]{2,1,0:T(8,128)(2,1)S(1)}, u32[]{:S(2)}, u32[]{:S(2)}) %all-to-all-start.7) | async-done | bytes 131104 | tf_op jit(solution)/shard_map/all_to_all | solution.py:46
  239.5 0.9 convolution_add_fusion
  (110 shorter events, 9.2 us)
Async XLA Ops:
  7.2 1.4 copy-start
  7.2 5.3 %copy-start.5 = (bf16[128,128]{1,0:T(8,128)(2,1)S(1)}, bf16[128,128]{1,0:T(8,128)(2,1)}, u32[]{:S(2)}) copy-start(bf16[128,128]{1,0:T(8,128)(2,1)} %param.11) | copy-start | bytes 98308
  7.2 5.3 %copy-start.9 = (s32[256]{0:T(256)S(1)}, s32[256]{0:T(256)}, u32[]{:S(2)}) copy-start(s32[256]{0:T(256)} %param.18) | copy-start | bytes 3076
  7.2 113.7 %all-gather.2.cloned.1.call-start = ((), (), s32[]{:S(2)}) async-start(), calls=%async_computation.8 | async-start | bytes 8257536 | tf_op jit(solution)/shard_map/all_gather | solution.py:85
  8.5 51.5 %copy-start.4 = (bf16[1024,512]{1,0:T(8,128)(2,1)S(1)}, bf16[1024,512]{1,0:T(8,128)(2,1)}, u32[]{:S(2)}) copy-start(bf16[1024,512]{1,0:T(8,128)(2,1)} %param.12) | copy-start | bytes 3145732
  12.4 88.5 %copy-start.13 = (s32[4,512]{1,0:T(4,128)S(1)}, s32[4,512]{1,0:T(4,128)}, u32[]{:S(2)}) copy-start(s32[4,512]{1,0:T(4,128)} %param.20) | copy-start | bytes 24580
  12.4 88.5 %copy-start.14 = (s32[4,512]{1,0:T(4,128)S(1)}, s32[4,512]{1,0:T(4,128)}, u32[]{:S(2)}) copy-start(s32[4,512]{1,0:T(4,128)} %param.19) | copy-start | bytes 24580
  12.5 106.9 %copy-start.6 = (s32[4,512]{1,0:T(4,128)S(1)}, s32[4,512]{1,0:T(4,128)}, u32[]{:S(2)}) copy-start(s32[4,512]{1,0:T(4,128)} %param.21) | copy-start | bytes 24580
  12.5 108.4 %copy-start.19 = (s32[128]{0:T(128)}, s32[128]{0:T(128)S(1)}, u32[]{:S(2)}) copy-start(s32[128]{0:T(128)S(1)} %iota_add_fusion) | copy-start | bytes 1540
  13.4 24.6 %all-to-all-start = ((bf16[64,4,128]{2,1,0:T(4,128)(2,1)}), bf16[64,4,128]{2,1,0:T(4,128)(2,1)S(1)}, u32[]{:S(2)}, u32[]{:S(2)}) async-start(bf16[64,4,128]{2,1,0:T(4,128)(2,1)} %bitcast), calls=%async_computation | async-start | bytes 131072 | tf_op jit(solution)/shard_map/all_to_all | solution.py:46
  28.3 33.6 %copy-start.21 = (bf16[136]{0:T(256)(128)(2,1)}, bf16[136]{0:T(256)(128)(2,1)S(1)}, u32[]{:S(2)}) copy-start(bf16[136]{0:T(256)(128)(2,1)S(1)} %pad.48.clone) | copy-start | bytes 820
  59.0 2.9 %copy-start.17 = (f32[136]{0:T(256)}, f32[136]{0:T(256)S(1)}, u32[]{:S(2)}) copy-start(f32[136]{0:T(256)S(1)} %add_rsqrt_fusion) | copy-start | bytes 1636
  61.2 59.8 %copy-start.8 = (bf16[136,512]{1,0:T(8,128)(2,1)}, bf16[136,512]{1,0:T(8,128)(2,1)S(1)}, u32[]{:S(2)}) copy-start(bf16[136,512]{1,0:T(8,128)(2,1)S(1)} %get-tuple-element.26) | copy-start | bytes 417796
  61.8 26.6 %all-to-all-start.1 = ((bf16[64,4,128]{2,1,0:T(4,128)(2,1)}), bf16[64,4,128]{2,1,0:T(4,128)(2,1)S(1)}, u32[]{:S(2)}, u32[]{:S(2)}) async-start(bf16[64,4,128]{2,1,0:T(4,128)(2,1)} %broadcast_in_dim.20), calls=%async_computation.1 | async-start | bytes 131072 | tf_op jit(solution)/shard_map/all_to_all | solution.py:46
  70.3 19.8 %copy-start.23 = (f32[256]{0:T(256)}, f32[256]{0:T(256)S(1)}, u32[]{:S(2)}) copy-start(f32[256]{0:T(256)S(1)} %add_convert_fusion) | copy-start | bytes 3076
  90.1 21.3 %all-to-all-start.2 = ((f32[64,4,128]{2,1,0:T(4,128)}), f32[64,4,128]{2,1,0:T(4,128)S(1)}, u32[]{:S(2)}, u32[]{:S(2)}) async-start(f32[64,4,128]{2,1,0:T(4,128)} %bitcast.2), calls=%async_computation.2 | async-start | bytes 262144 | tf_op jit(solution)/shard_map/all_to_all | solution.py:46
  111.6 7.8 %copy-start.7 = (f32[4,128]{1,0:T(4,128)}, f32[4,128]{1,0:T(4,128)S(1)}, u32[]{:S(2)}) copy-start(f32[4,128]{1,0:T(4,128)S(1)} %get-tuple-element.9) | copy-start | bytes 6148
  111.6 7.8 %copy-start.15 = (f32[4]{0:T(128)}, f32[4]{0:T(128)S(1)}, u32[]{:S(2)}) copy-start(f32[4]{0:T(128)S(1)} %broadcast_multiply_fusion.7) | copy-start | bytes 52
  111.8 7.6 %copy-start.16 = (f32[4]{0:T(128)}, f32[4]{0:T(128)S(1)}, u32[]{:S(2)}) copy-start(f32[4]{0:T(128)S(1)} %add_rsqrt_fusion.1) | copy-start | bytes 52
  111.9 7.5 %copy-start.11 = (bf16[4,128]{1,0:T(4,128)(2,1)}, bf16[4,128]{1,0:T(4,128)(2,1)S(1)}, u32[]{:S(2)}) copy-start(bf16[4,128]{1,0:T(4,128)(2,1)S(1)} %fusion.73) | copy-start | bytes 3076
  112.5 14.6 %all-to-all-start.3 = ((bf16[8,4,128]{2,1,0:T(4,128)(2,1)}), bf16[8,4,128]{2,1,0:T(4,128)(2,1)S(1)}, u32[]{:S(2)}, u32[]{:S(2)}) async-start(bf16[8,4,128]{2,1,0:T(4,128)(2,1)} %broadcast_in_dim.22), calls=%async_computation.3 | async-start | bytes 16384 | tf_op jit(solution)/shard_map/all_to_all | solution.py:46
  122.2 7.8 %copy-start.1 = (bf16[8,128,512]{2,1,0:T(8,128)(2,1)}, bf16[8,128,512]{2,1,0:T(8,128)(2,1)S(1)}, u32[]{:S(2)}) copy-start(bf16[8,128,512]{2,1,0:T(8,128)(2,1)S(1)} %slice.199) | copy-start | bytes 3145732
  143.5 6.8 %copy-start.12 = (f32[512]{0:T(512)S(1)}, f32[512]{0:T(512)}, u32[]{:S(2)}) copy-start(f32[512]{0:T(512)} %param.17) | copy-start | bytes 6148
  143.5 6.8 %copy-start.2 = (bf16[8,128,512]{2,1,0:T(8,128)(2,1)S(1)}, bf16[8,128,512]{2,1,0:T(8,128)(2,1)}, u32[]{:S(2)}) copy-start(bf16[8,128,512]{2,1,0:T(8,128)(2,1)} %copy-done.1) | copy-start | bytes 3145732
  173.9 11.3 %copy-start.18 = (f32[136]{0:T(256)S(1)}, f32[136]{0:T(256)}, u32[]{:S(2)}) copy-start(f32[136]{0:T(256)} %copy-done.17) | copy-start | bytes 1636
  173.9 11.3 %copy-start.3 = (f32[136,1024]{1,0:T(8,128)S(1)}, f32[136,1024]{1,0:T(8,128)}, u32[]{:S(2)}) copy-start(f32[136,1024]{1,0:T(8,128)} %get-tuple-element.23) | copy-start | bytes 1671172
  176.1 9.6 %slice-start = ((f32[136]{0:T(256)}), f32[128]{0:T(128)S(1)}, s32[]{:S(2)}) async-start(f32[136]{0:T(256)} %copy-done.17), calls=%async_computation.9 | async-start | bytes 1024 | tf_op jit(solution)/shard_map/slice | solution.py:191
  178.4 26.8 %copy-start.22 = (bf16[136]{0:T(256)(128)(2,1)S(1)}, bf16[136]{0:T(256)(128)(2,1)}, u32[]{:S(2)}) copy-start(bf16[136]{0:T(256)(128)(2,1)} %copy-done.21) | copy-start | bytes 820
  178.4 25.5 %all-to-all-start.5 = ((bf16[64,36,128]{2,1,0:T(8,128)(2,1)}), bf16[64,36,128]{2,1,0:T(8,128)(2,1)S(1)}, u32[]{:S(2)}, u32[]{:S(2)}) async-start(bf16[64,36,128]{2,1,0:T(8,128)(2,1)} %pad_maximum_fusion.1), calls=%async_computation.5 | async-start | bytes 1310720 | tf_op jit(solution)/shard_map/all_to_all | solution.py:46
  183.9 55.6 %copy-start.10 = (s32[256]{0:T(256)S(1)}, s32[256]{0:T(256)}, u32[]{:S(2)}) copy-start(s32[256]{0:T(256)} %param.18) | copy-start | bytes 3076
  183.9 55.5 %copy-start.20 = (s32[128]{0:T(128)S(1)}, s32[128]{0:T(128)}, u32[]{:S(2)}) copy-start(s32[128]{0:T(128)} %copy-done.19) | copy-start | bytes 1540
  206.0 16.3 %all-to-all-start.6 = ((bf16[8,136,128]{2,1,0:T(8,128)(2,1)}), bf16[8,136,128]{2,1,0:T(8,128)(2,1)S(1)}, u32[]{:S(2)}, u32[]{:S(2)}) async-start(bf16[8,136,128]{2,1,0:T(8,128)(2,1)} %maximum_bitcast_fusion), calls=%async_computation.6 | async-start | bytes 557056 | tf_op jit(solution)/shard_map/all_to_all | solution.py:46
  223.1 16.2 %all-to-all-start.7 = ((bf16[64,8,128]{2,1,0:T(8,128)(2,1)}), bf16[64,8,128]{2,1,0:T(8,128)(2,1)S(1)}, u32[]{:S(2)}, u32[]{:S(2)}) async-start(bf16[64,8,128]{2,1,0:T(8,128)(2,1)} %broadcast_in_dim.26), calls=%async_computation.7 | async-start | bytes 262144 | tf_op jit(solution)/shard_map/all_to_all | solution.py:46
Sparse Core Ops, SparseCore 0:
  12.6 87.2 all-gather.1

commit v2 on v1

v2 whole, which is shorter than its diff:
```python
import functools

import jax
import jax.numpy as jnp
from jax import lax
from jax.experimental import pallas as pl
from jax.experimental.pallas import tpu as pltpu
from jax.sharding import PartitionSpec as P

HEAD = 128
norm_eps = 1e-05
F32 = jnp.float32
BF16 = jnp.bfloat16
PAD = 16
CHUNK = 128


def sigmoid_slope(argument):
    part = jax.nn.sigmoid(argument)
    return argument * part, part * (1.0 + argument * (1.0 - part))


def layer_norm(argument):
    centred = argument - jnp.mean(argument, -1, keepdims=True)
    inverse = lax.rsqrt(jnp.mean(centred * centred, -1, keepdims=True) + norm_eps)
    return (centred * inverse, inverse)


def norm_back(gradient, normed, inverse):
    return inverse * (
        gradient
        - jnp.mean(gradient, -1, keepdims=True)
        - normed * jnp.mean(gradient * normed, -1, keepdims=True)
    )


def mm(left, right, dims=((1,), (0,))):
    return lax.dot_general(left, right, (dims, ((), ())), preferred_element_type=F32)


def mm_split(left, right, dims=((1,), (0,))):
    high = left.astype(BF16)
    rest = left - high.astype(F32)
    middle = rest.astype(BF16)
    low = (rest - middle.astype(F32)).astype(BF16)
    count = left.shape[0]
    product = mm(jnp.concatenate([high, middle, low], 0), right, dims)
    return product[:count] + product[count : 2 * count] + product[2 * count :]


def swap(block, axis):
    return lax.all_to_all(block, axis, 0, 0, tiled=True)


def send_all(block, axis, size):
    return swap(jnp.broadcast_to(block[None], (size,) + block.shape), axis)


def score_kernel(
    count,
    request_ref,
    gated_ref,
    merge_ref,
    user_ref,
    item_ref,
    weight_ref,
    owner_ref,
    row_ref,
    target_ref,
    cand_ref,
    out_ref,
    user_proj,
):
    heads = gated_ref.shape[0]
    gated = jnp.concatenate([gated_ref[head] for head in range(heads)], 1)
    layer_out = request_ref[...].astype(F32) + mm(gated, merge_ref[...])
    user_proj[...] = mm(layer_out.astype(BF16), user_ref[...])
    slots, hidden = owner_ref.shape[0], user_ref.shape[1]
    table_rows = item_ref.shape[0]
    weights = weight_ref[...]
    out_ref[...] = jnp.zeros_like(out_ref)
    lanes = lax.broadcasted_iota(jnp.int32, (CHUNK, table_rows), 1)
    for request in range(count):
        user_row = user_proj[request : request + 1, :]

        def step(index, sums, request=request, user_row=user_row):
            begin = pl.multiple_of(index * CHUNK, CHUNK)
            owned = owner_ref[pl.ds(begin, CHUNK), request : request + 1] == cand_ref[0]
            place = row_ref[pl.ds(begin, CHUNK), request : request + 1]
            target = target_ref[pl.ds(begin, CHUNK), request : request + 1]
            chosen = jnp.where(lanes == place, 1.0, 0.0).astype(BF16)
            pre_score = mm(chosen, item_ref[...]) + user_row
            part = 0.5 + 0.5 * jnp.tanh(0.5 * pre_score)
            smooth = pre_score * part
            slope = part + smooth * (1.0 - part)
            scores = jnp.sum(smooth * weights, -1, keepdims=True)
            power = jnp.where(owned, jnp.exp(scores), 0.0)
            target = jnp.where(owned, target, 0.0)
            soft = (0.25 * power * slope).reshape(-1, 8, hidden)
            hard = (target * slope).reshape(-1, 8, hidden)
            scalars = jnp.where(
                lax.broadcasted_iota(jnp.int32, (CHUNK, HEAD), 1) == 0, power, target * scores
            )
            return (
                sums[0] + jnp.sum(soft, 0),
                sums[1] + jnp.sum(hard, 0),
                sums[2] + jnp.sum(scalars.reshape(-1, 8, HEAD), 0),
            )

        zero = jnp.zeros((8, hidden), F32)
        sums = lax.fori_loop(
            0, slots // CHUNK, step, (zero, zero, jnp.zeros((8, HEAD), F32)), unroll=2
        )
        out_ref[request : request + 1, :hidden] = jnp.sum(sums[0], 0, keepdims=True)
        out_ref[request : request + 1, hidden : 2 * hidden] = jnp.sum(sums[1], 0, keepdims=True)
        out_ref[request : request + 1, 2 * hidden :] = jnp.sum(sums[2], 0, keepdims=True)


def score_parts(count, cand, request_rows, gated, merge, user, items, weights, owner, row, target):
    vmem = pl.BlockSpec(memory_space=pltpu.VMEM)
    hidden = user.shape[1]
    return pl.pallas_call(
        functools.partial(score_kernel, count),
        out_shape=jax.ShapeDtypeStruct((8, 2 * hidden + HEAD), F32),
        in_specs=[vmem] * 9 + [pl.BlockSpec(memory_space=pltpu.SMEM)],
        out_specs=vmem,
        scratch_shapes=[pltpu.VMEM((PAD, hidden), F32)],
        compiler_params=pltpu.CompilerParams(vmem_limit_bytes=48 * 1024 * 1024),
        cost_estimate=pl.CostEstimate(
            flops=3 * 10**9, bytes_accessed=5 * 10**6, transcendentals=10**6
        ),
    )(request_rows, gated, merge, user, items, weights, owner, row, target, cand)


def per_device(
    n_ctx,
    n_cand,
    history,
    head_weights,
    merge_weights,
    cand_table,
    user_weights,
    item_weights,
    score_weights,
    request_points,
    candidate_owner,
    candidate_row,
    relevance,
):
    rows, width = history.shape
    requests = request_points.shape[0]
    own = requests // n_ctx
    features = width * n_cand
    hidden = user_weights.shape[1]
    strip = features // n_ctx
    ctx = lax.axis_index("ctx")
    cand = lax.axis_index("cand")
    first_row = ctx * rows
    scaling = HEAD ** (-0.5)

    riding = lax.all_gather(
        jnp.concatenate([history, user_weights], 1), "cand", axis=0, tiled=False
    )
    merge_full = lax.all_gather(merge_weights, "cand", axis=0, tiled=True)

    positions = first_row + jnp.arange(rows, dtype=jnp.int32)
    matches = (request_points[:, None] == positions[None, :]).astype(BF16)
    picked = mm(matches, history).astype(BF16).reshape(n_ctx, own, width)
    picked = swap(picked, "ctx")
    picked = jnp.sum(picked.astype(F32), 0).astype(BF16)

    picked = send_all(jnp.pad(picked, ((0, PAD - own), (0, 0))), "cand", n_cand)
    picked = picked.transpose(1, 0, 2).reshape(PAD, features)
    r_normed, r_inverse = layer_norm(picked.astype(F32))
    request_low = r_normed.astype(BF16)
    weights_request = jnp.concatenate(
        [head_weights[:, :HEAD], head_weights[:, 2 * HEAD : 3 * HEAD]], 1
    )
    before_request = mm(request_low, weights_request)
    smooth, slope_request = sigmoid_slope(before_request)
    gate = smooth[:own, :HEAD].astype(BF16).astype(F32)
    own_queries = smooth[:own, HEAD:].astype(BF16)

    x_wide = riding[:, :, :width].transpose(1, 0, 2).reshape(rows, features).astype(F32)
    user_full = riding[:, :, width:].reshape(features, hidden)
    x_normed, x_inverse = layer_norm(x_wide)
    x_low = x_normed.astype(BF16)
    weights_dense = jnp.concatenate(
        [head_weights[:, HEAD : 2 * HEAD], head_weights[:, 3 * HEAD :]], 1
    )
    before = mm(x_low, weights_dense)
    smooth, slope = sigmoid_slope(before)
    values = smooth[:, :HEAD].astype(BF16)
    key_heads = smooth[:, HEAD:].astype(BF16)

    queries = send_all(own_queries, "ctx", n_ctx).reshape(requests, HEAD)
    logits = mm(queries, key_heads, ((1,), (1,))) * scaling
    allowed = positions[None, :] <= request_points[:, None]
    divisor = (request_points + 1).astype(F32)[:, None]
    logit_smooth, logit_slope = sigmoid_slope(logits)
    weight = jnp.where(allowed, logit_smooth / divisor, 0.0).astype(BF16)
    attended = swap(mm(weight, values).reshape(n_ctx, own, HEAD), "ctx")
    attended = jnp.sum(attended, 0)
    normed, inverse = layer_norm(attended)
    gated = (normed * gate).astype(BF16)

    item_proj = mm(cand_table, item_weights).astype(BF16)
    target = (relevance + 1).astype(F32)
    target = target / jnp.sum(target, -1, keepdims=True)
    gated, merge_full, user_full = lax.optimization_barrier((gated, merge_full, user_full))
    gated_full = send_all(jnp.pad(gated, ((0, PAD - own), (0, 0))), "cand", n_cand)
    parts = score_parts(
        own,
        cand[None],
        picked,
        gated_full,
        merge_full,
        user_full,
        item_proj,
        score_weights[None],
        candidate_owner.T,
        candidate_row.T,
        target.T,
    )
    parts = jnp.sum(send_all(parts[:own], "cand", n_cand).reshape(n_cand, own, -1), 0)
    total = parts[:, 2 * hidden : 2 * hidden + 1]
    losses = jnp.log(total[:, 0]) - parts[:, 2 * hidden + 1]
    d_user = parts[:, :hidden] / (0.25 * total) - parts[:, hidden : 2 * hidden]
    d_user = d_user * score_weights
    d_picked = mm_split(d_user, user_full, ((1,), (1,)))
    d_gated = mm_split(d_picked, merge_weights, ((1,), (1,)))
    d_attended = norm_back(d_gated * gate, normed, inverse).astype(BF16)
    d_before_gate = (d_gated * normed * slope_request[:own, :HEAD]).astype(BF16)

    blocks = features // HEAD
    strips = jnp.concatenate(
        [
            request_low[:own].reshape(own, blocks, HEAD).transpose(1, 0, 2),
            d_picked.astype(BF16).reshape(own, blocks, HEAD).transpose(1, 0, 2),
        ],
        1,
    )
    strips = jnp.repeat(strips, n_ctx // blocks, axis=0)
    shared = jnp.concatenate([d_attended, gated, d_before_gate], 0)
    sent = jnp.concatenate(
        [jnp.broadcast_to(shared[None], (n_ctx,) + shared.shape), strips], 1
    )
    sent = swap(sent, "ctx")
    all_grads = sent[:, :own].reshape(requests, HEAD)
    all_gated = sent[:, own : 2 * own].reshape(requests, HEAD)
    all_gate_grads = sent[:, 2 * own : 3 * own].reshape(requests, HEAD)
    x_block = sent[:, 3 * own : 4 * own].reshape(requests, HEAD)
    d_block = sent[:, 4 * own :].reshape(requests, HEAD)
    lane = lax.rem(ctx, n_ctx // blocks) * strip
    grad_merge = mm(d_block, all_gated, ((0,), (0,)))
    grad_merge = lax.dynamic_slice_in_dim(grad_merge, lane, strip, 0).T
    slopes = mm(all_grads, values, ((1,), (1,)))
    d_logit = jnp.where(allowed, slopes * logit_slope / divisor, 0.0).astype(BF16)
    d_query = (mm(d_logit, key_heads) * scaling).astype(BF16)
    d_key = mm(d_logit, queries, ((0,), (0,))) * scaling
    d_value = mm(weight, all_grads, ((0,), (0,)))
    d_value = (d_value * slope[:, :HEAD]).astype(BF16)
    d_key = (d_key * slope[:, HEAD:]).astype(BF16)
    dense = jnp.concatenate([d_value, d_key], 1)
    dense_grad = mm(x_low, dense, ((0,), (0,))).astype(BF16)
    dense_grad = dense_grad.reshape(n_ctx, strip, 2 * HEAD)
    dense_grad = jnp.concatenate(
        [dense_grad[:, :, :HEAD], dense_grad[:, :, HEAD:], d_query.reshape(n_ctx, own, HEAD)], 1
    )
    dense_grad = jnp.sum(swap(dense_grad, "ctx").astype(F32), 0)
    own_query_grad = dense_grad[2 * strip :]
    d_before_query = (own_query_grad * slope_request[:own, HEAD:]).astype(BF16)

    back_dense = norm_back(mm(dense, weights_dense, ((1,), (1,))), x_normed, x_inverse)
    back_dense = lax.psum_scatter(
        back_dense.reshape(rows, n_cand, width).transpose(1, 0, 2).reshape(n_cand * rows, width),
        "cand",
        scatter_dimension=0,
        tiled=True,
    )
    request_before = jnp.concatenate([d_before_gate, d_before_query], 1)
    back = norm_back(
        mm(request_before, weights_request, ((1,), (1,))), r_normed[:own], r_inverse[:own]
    )
    back = back.reshape(own, n_cand, width).transpose(1, 0, 2)
    back = jnp.sum(swap(back, "cand"), 0)
    own_slice = lax.dynamic_slice_in_dim(d_picked, cand * width, width, 1)
    request_grad = back + own_slice
    final = jnp.concatenate([request_grad.astype(BF16), d_before_query], 0)
    final = send_all(final, "ctx", n_ctx)
    all_request_grad = final[:, :own].reshape(requests, width)
    all_query_grads = final[:, own:].reshape(requests, HEAD)
    history_grad = back_dense + mm(matches, all_request_grad, ((0,), (0,)))
    gate_query = mm(
        x_block, jnp.concatenate([all_gate_grads, all_query_grads], 1), ((0,), (0,))
    )
    gate_query = lax.dynamic_slice_in_dim(gate_query, lane, strip, 0)
    grad_heads = jnp.concatenate(
        [
            gate_query[:, :HEAD],
            dense_grad[:strip],
            gate_query[:, HEAD:],
            dense_grad[strip : 2 * strip],
        ],
        1,
    )
    return (losses, history_grad, grad_heads, grad_merge)


def solution(mesh):
    n_ctx = mesh.shape["ctx"]
    n_cand = mesh.shape["cand"]

    def body(*args):
        return per_device(n_ctx, n_cand, *args)

    return jax.shard_map(
        body,
        mesh=mesh,
        in_specs=(
            P("ctx", "cand"),
            P(None, "cand"),
            P("cand", None),
            P("cand", None),
            P("cand", None),
            P(),
            P(),
            P(),
            P("ctx", None),
            P("ctx", None),
            P("ctx", None),
        ),
        out_specs=(P("ctx"), P("ctx", "cand"), P("ctx", "cand"), P("cand", "ctx")),
        check_vma=False,
    )
```

time: 249 us -> 224 us (0.90)
  blocking collectives: 37.7 us -> 24.7 us
  local copies, waits for them, and re-layouts: 19.8 us -> 9.48 us
  Pallas kernels: 0 us -> 6.85 us
  other arithmetic: 19 us -> 12.6 us
  matrix products: 18.1 us -> 13.7 us
    all_gather x1 -> x0, blocking collectives: 20.4 us -> none  [per_device(): lax.all_gather(jnp.concatenate([history, picked, pad], 0), 'cand', axis=1...]
    gather x1 -> x0, local copies, waits for them, and re-layouts: 12.6 us -> none  [per_device(): items = table[place].astype(F32)]
    all_to_all x1, blocking collectives: 17.3 us -> 24.7 us  [swap(): return lax.all_to_all(block, axis, 0, 0, tiled=True)]
    pallas_call x0 -> x1, Pallas kernels: none -> 6.85 us  [score_parts(): pl.pallas_call(functools.partial(score_kernel, count), out_shape=jax.Shap...]
    reduce_sum x4 -> x2, other arithmetic: 5.49 us -> 0.05 us  [the longest x1 0.03 us: per_device(): jnp.sum(send_all(parts[:own], 'cand', n_cand).reshape(n_cand, own, -1), 0)]
    dot_general x20 -> x18, matrix products: 18.1 us -> 13.7 us  [mm(): lax.dot_general(left, right, (dims, ((), ())), preferred_element_type=F32)]
    unnamed x50 -> x102, local copies, waits for them, and re-layouts: 0.38 us -> 2.89 us
    all_to_all x7 -> x9, waiting for transfers between devices: 82.9 us -> 84.5 us  [swap(): return lax.all_to_all(block, axis, 0, 0, tiled=True)]
  transfers between devices with their start and end apart: 8 -> 12, of which waited for: 7 -> 9; matrix products, arithmetic and copies ran while one was open for 5% -> 10% of each run, Pallas kernels for 0% -> 0%
where the time goes in v2:
time: 224 us; the launch traced here: 222 us
  waiting for transfers between devices  85.3 us (38%)
  starting transfers between devices  55.1 us (25%)
  blocking collectives  24.7 us (11%)
  between operations  14.7 us (7%)
  matrix products  13.7 us (6%)
  other arithmetic  12.6 us (6%)
  local copies, waits for them, and re-layouts  9.48 us (4%)
  Pallas kernels  6.85 us (3%)
    all_to_all x9, waiting for transfers between devices, swap(): return lax.all_to_all(block, axis, 0, 0, tiled=True)  84.5 us
    all_to_all x9, starting transfers between devices, swap(): return lax.all_to_all(block, axis, 0, 0, tiled=True)  55 us
    all_to_all x1, blocking collectives, swap(): return lax.all_to_all(block, axis, 0, 0, tiled=True)  24.7 us
    dot_general x18, matrix products, mm(): lax.dot_general(left, right, (dims, ((), ())), preferred_element_type=F32)  13.7 us
    pallas_call x1, Pallas kernels, score_parts(): pl.pallas_call(functools.partial(score_kernel, count), out_shape=jax.Shap...  6.85 us
  transfers between devices with their start and end apart: 12, of which 9 were waited for; matrix products, arithmetic and copies ran while one was open for 10% of the time, Pallas kernels for 0%

profile of v2, /device:TPU:8, one launch (start us, length us, event | category | flops | bytes accessed | tf_op | source)
XLA Modules:
  0.0 222.3 jit_solution(11180255486371089301)
XLA Ops:
  7.2 1.7 pad_maximum_fusion.8
  9.0 1.6 convolution_convert_fusion.2
  10.6 14.8 %all-to-all-start = ((bf16[64,4,128]{2,1,0:T(4,128)(2,1)}), bf16[64,4,128]{2,1,0:T(4,128)(2,1)S(1)}, u32[]{:S(2)}, u32[]{:S(2)}) async-start(bf16[64,4,128]{2,1,0:T(4,128)(2,1)} %bitcast), calls=%async_computation | async-start | bytes 131072 | tf_op jit(solution)/shard_map/all_to_all | solution.py:52
  25.5 0.7 all-gather.4.cloned.1.call-update
  26.2 1.3 fusion.75
  27.7 7.5 %all-to-all-done = bf16[64,4,128]{2,1,0:T(4,128)(2,1)S(1)} async-done(((bf16[64,4,128]{2,1,0:T(4,128)(2,1)}), bf16[64,4,128]{2,1,0:T(4,128)(2,1)S(1)}, u32[]{:S(2)}, u32[]{:S(2)}) %all-to-all-start) | async-done | bytes 65568 | tf_op jit(solution)/shard_map/all_to_all | solution.py:52
  35.3 0.6 broadcast_in_dim.23
  35.9 6.2 %all-to-all-start.1 = ((bf16[8,16,128]{2,1,0:T(8,128)(2,1)}), bf16[8,16,128]{2,1,0:T(8,128)(2,1)S(1)}, u32[]{:S(2)}, u32[]{:S(2)}) async-start(bf16[8,16,128]{2,1,0:T(8,128)(2,1)} %broadcast_in_dim.23), calls=%async_computation.1 | async-start | bytes 65536 | tf_op jit(solution)/shard_map/all_to_all | solution.py:52
  42.6 7.3 %all-to-all-done.1 = bf16[8,16,128]{2,1,0:T(8,128)(2,1)S(1)} async-done(((bf16[8,16,128]{2,1,0:T(8,128)(2,1)}), bf16[8,16,128]{2,1,0:T(8,128)(2,1)S(1)}, u32[]{:S(2)}, u32[]{:S(2)}) %all-to-all-start.1) | async-done | bytes 32800 | tf_op jit(solution)/shard_map/all_to_all | solution.py:52
  50.3 0.7 subtract_multiply_fusion
  51.0 0.8 add_multiply_fusion.1
  51.8 0.6 broadcast_in_dim.24
  52.5 5.8 %all-to-all-start.2 = ((bf16[64,4,128]{2,1,0:T(4,128)(2,1)}), bf16[64,4,128]{2,1,0:T(4,128)(2,1)S(1)}, u32[]{:S(2)}, u32[]{:S(2)}) async-start(bf16[64,4,128]{2,1,0:T(4,128)(2,1)} %broadcast_in_dim.24), calls=%async_computation.2 | async-start | bytes 131072 | tf_op jit(solution)/shard_map/all_to_all | solution.py:52
  58.3 1.1 convert_reduce_fusion.1
  59.4 1.2 fusion.8
  60.6 1.9 add_multiply_fusion
  62.5 5.6 %all-to-all-done.2 = bf16[64,4,128]{2,1,0:T(4,128)(2,1)S(1)} async-done(((bf16[64,4,128]{2,1,0:T(4,128)(2,1)}), bf16[64,4,128]{2,1,0:T(4,128)(2,1)S(1)}, u32[]{:S(2)}, u32[]{:S(2)}) %all-to-all-start.2) | async-done | bytes 65568 | tf_op jit(solution)/shard_map/all_to_all | solution.py:52
  68.1 0.9 fusion.17
  69.0 0.8 fusion.37
  69.8 5.9 %all-to-all-start.3 = ((f32[64,4,128]{2,1,0:T(4,128)}), f32[64,4,128]{2,1,0:T(4,128)}, u32[]{:S(2)}, u32[]{:S(2)}) async-start(f32[64,4,128]{2,1,0:T(4,128)} %bitcast.5), calls=%async_computation.3 | async-start | bytes 262144 | tf_op jit(solution)/shard_map/all_to_all | solution.py:52
  75.7 2.1 convolution_convert_fusion.1.item_ref
  77.9 12.4 %all-to-all-done.3 = f32[64,4,128]{2,1,0:T(4,128)} async-done(((f32[64,4,128]{2,1,0:T(4,128)}), f32[64,4,128]{2,1,0:T(4,128)}, u32[]{:S(2)}, u32[]{:S(2)}) %all-to-all-start.3) | async-done | bytes 131104 | tf_op jit(solution)/shard_map/all_to_all | solution.py:52
  90.4 1.1 fusion.70
  91.8 0.6 broadcast_in_dim.26
  92.4 3.3 %all-to-all-start.4 = ((bf16[8,16,128]{2,1,0:T(8,128)(2,1)}), bf16[8,16,128]{2,1,0:T(8,128)(2,1)S(1)}, u32[]{:S(2)}, u32[]{:S(2)}) async-start(bf16[8,16,128]{2,1,0:T(8,128)(2,1)} %broadcast_in_dim.26), calls=%async_computation.4 | async-start | bytes 65536 | tf_op jit(solution)/shard_map/all_to_all | solution.py:52
  95.8 7.8 %all-to-all-done.4.gated_ref = bf16[8,16,128]{2,1,0:T(8,128)(2,1)S(1)} async-done(((bf16[8,16,128]{2,1,0:T(8,128)(2,1)}), bf16[8,16,128]{2,1,0:T(8,128)(2,1)S(1)}, u32[]{:S(2)}, u32[]{:S(2)}) %all-to-all-start.4) | async-done | bytes 32800 | tf_op jit(solution)/shard_map/all_to_all | solution.py:52
  103.6 1.6 copy-done.2
  105.2 6.8 %shard_map.138 = f32[8,1152]{1,0:T(8,128)S(1)} custom-call(bf16[16,1024]{1,0:T(8,128)(2,1)S(1)} %copy_bitcast_fusion.request_ref, bf16[8,16,128]{2,1,0:T(8,128)(2,1)S(1)} %all-to-all-done.4.gated_ref, bf16[1024,1024]{1,0:T(8,128)(2,1)S(1)} %copy-done.2, bf16[1024,512]{1,0:T(8,128)(2,1)S(1)} %bitcast.98, ...), custom_call_target="tpu_custom_call" | custom-call | flops 3000000000 | bytes 5000000 | tf_op jit(solution)/shard_map/pallas_call | solution.py:122
  112.1 0.7 broadcast_in_dim.29
  112.8 3.4 %all-to-all-start.5 = ((f32[8,4,1152]{2,1,0:T(4,128)}), f32[8,4,1152]{2,1,0:T(4,128)S(1)}, u32[]{:S(2)}, u32[]{:S(2)}) async-start(f32[8,4,1152]{2,1,0:T(4,128)} %broadcast_in_dim.29), calls=%async_computation.5 | async-start | bytes 294912 | tf_op jit(solution)/shard_map/all_to_all | solution.py:52
  116.2 9.4 %all-to-all-done.5 = f32[8,4,1152]{2,1,0:T(4,128)S(1)} async-done(((f32[8,4,1152]{2,1,0:T(4,128)}), f32[8,4,1152]{2,1,0:T(4,128)S(1)}, u32[]{:S(2)}, u32[]{:S(2)}) %all-to-all-start.5) | async-done | bytes 147488 | tf_op jit(solution)/shard_map/all_to_all | solution.py:52
  125.6 0.7 multiply_reduce_fusion.3
  127.0 0.9 fusion.57
  128.0 0.8 multiply_convert_fusion.2
  129.3 24.7 %all_to_all.50 = bf16[64,20,128]{2,1,0:T(8,128)(2,1)S(1)} all-to-all(bf16[64,20,128]{2,1,0:T(8,128)(2,1)S(1)} %pad_maximum_fusion.3), channel_id=1, replica_groups=mesh['ctx'=64,'cand'=8] {'ctx'}, dimensions={0} | all-to-all | bytes 655360 | tf_op jit(solution)/shard_map/all_to_all | solution.py:52
  155.9 0.9 pad_maximum_fusion
  156.8 5.8 %all-to-all-start.7 = ((bf16[64,36,128]{2,1,0:T(8,128)(2,1)}), bf16[64,36,128]{2,1,0:T(8,128)(2,1)S(1)}, u32[]{:S(2)}, u32[]{:S(2)}) async-start(bf16[64,36,128]{2,1,0:T(8,128)(2,1)} %pad_maximum_fusion), calls=%async_computation.8 | async-start | bytes 1310720 | tf_op jit(solution)/shard_map/all_to_all | solution.py:52
  162.8 1.4 fusion.69
  164.6 0.9 copy.109
  165.6 17.0 %all-to-all-done.7 = bf16[64,36,128]{2,1,0:T(8,128)(2,1)S(1)} async-done(((bf16[64,36,128]{2,1,0:T(8,128)(2,1)}), bf16[64,36,128]{2,1,0:T(8,128)(2,1)S(1)}, u32[]{:S(2)}, u32[]{:S(2)}) %all-to-all-start.7) | async-done | bytes 589856 | tf_op jit(solution)/shard_map/all_to_all | solution.py:52
  182.8 0.7 fusion.51
  183.9 0.7 multiply_bitcast_fusion.1
  184.6 3.3 %all-to-all-start.8 = ((f32[8,4,128]{2,1,0:T(4,128)}), f32[8,4,128]{2,1,0:T(4,128)S(1)}, u32[]{:S(2)}, u32[]{:S(2)}) async-start(f32[8,4,128]{2,1,0:T(4,128)} %multiply_bitcast_fusion.1), calls=%async_computation.9 | async-start | bytes 32768 | tf_op jit(solution)/shard_map/all_to_all | solution.py:52
  188.1 7.6 %all-to-all-done.8 = f32[8,4,128]{2,1,0:T(4,128)S(1)} async-done(((f32[8,4,128]{2,1,0:T(4,128)}), f32[8,4,128]{2,1,0:T(4,128)S(1)}, u32[]{:S(2)}, u32[]{:S(2)}) %all-to-all-start.8) | async-done | bytes 16416 | tf_op jit(solution)/shard_map/all_to_all | solution.py:52
  195.8 0.7 broadcast_in_dim.32
  196.4 6.3 %all-to-all-start.9 = ((bf16[64,8,128]{2,1,0:T(8,128)(2,1)}), bf16[64,8,128]{2,1,0:T(8,128)(2,1)S(1)}, u32[]{:S(2)}, u32[]{:S(2)}) async-start(bf16[64,8,128]{2,1,0:T(8,128)(2,1)} %broadcast_in_dim.32), calls=%async_computation.10 | async-start | bytes 262144 | tf_op jit(solution)/shard_map/all_to_all | solution.py:52
  203.4 9.8 %all-to-all-done.9 = bf16[64,8,128]{2,1,0:T(8,128)(2,1)S(1)} async-done(((bf16[64,8,128]{2,1,0:T(8,128)(2,1)}), bf16[64,8,128]{2,1,0:T(8,128)(2,1)S(1)}, u32[]{:S(2)}, u32[]{:S(2)}) %all-to-all-start.9) | async-done | bytes 131104 | tf_op jit(solution)/shard_map/all_to_all | solution.py:52
  214.0 1.8 convolution_add_fusion
  (170 shorter events, 7.3 us)
Async XLA Ops:
  7.2 68.6 %copy-start = (bf16[512,1024]{1,0:T(8,128)(2,1)S(1)}, bf16[512,1024]{1,0:T(8,128)(2,1)}, u32[]{:S(2)}) copy-start(bf16[512,1024]{1,0:T(8,128)(2,1)} %param.14) | copy-start | bytes 3145732
  7.2 51.1 %all-gather.6.cloned.1.call-start = ((), (), s32[]{:S(2)}) async-start(), calls=%async_computation.13 | async-start | bytes 1474560 | tf_op jit(solution)/shard_map/all_gather | solution.py:161
  8.9 18.6 %copy-start.23 = (s32[4,512]{1,0:T(4,128)S(1)}, s32[4,512]{1,0:T(4,128)}, u32[]{:S(2)}) copy-start(s32[4,512]{1,0:T(4,128)} %param.21) | copy-start | bytes 24580
  9.0 59.2 %copy-start.37 = (s32[128]{0:T(128)}, s32[128]{0:T(128)S(1)}, u32[]{:S(2)}) copy-start(s32[128]{0:T(128)S(1)} %iota_add_fusion) | copy-start | bytes 1540
  10.6 24.6 %all-to-all-start = ((bf16[64,4,128]{2,1,0:T(4,128)(2,1)}), bf16[64,4,128]{2,1,0:T(4,128)(2,1)S(1)}, u32[]{:S(2)}, u32[]{:S(2)}) async-start(bf16[64,4,128]{2,1,0:T(4,128)(2,1)} %bitcast), calls=%async_computation | async-start | bytes 131072 | tf_op jit(solution)/shard_map/all_to_all | solution.py:52
  25.4 16.7 %copy-start.24 = (s32[256]{0:T(256)S(1)}, s32[256]{0:T(256)}, u32[]{:S(2)}) copy-start(s32[256]{0:T(256)} %param.18) | copy-start | bytes 3076
  25.4 66.4 %all-gather.4.cloned.1.call-start = ((), (), s32[]{:S(2)}) async-start(), calls=%async_computation.11 | async-start | bytes 2359296 | tf_op jit(solution)/shard_map/all_gather | solution.py:164
  26.2 16.2 %copy-start.26 = (s32[4,512]{1,0:T(4,128)S(1)}, s32[4,512]{1,0:T(4,128)}, u32[]{:S(2)}) copy-start(s32[4,512]{1,0:T(4,128)} %param.19) | copy-start | bytes 24580
  26.2 16.3 %copy-start.27 = (s32[4,512]{1,0:T(4,128)S(1)}, s32[4,512]{1,0:T(4,128)}, u32[]{:S(2)}) copy-start(s32[4,512]{1,0:T(4,128)} %param.20) | copy-start | bytes 24580
  27.5 25.0 %copy-start.10 = (bf16[1024,128]{1,0:T(8,128)(2,1)}, bf16[1024,128]{1,0:T(8,128)(2,1)S(1)}, u32[]{:S(2)}) copy-start(bf16[1024,128]{1,0:T(8,128)(2,1)S(1)} %get-tuple-element.26) | copy-start | bytes 786436
  27.5 33.1 %copy-start.12 = (bf16[1024,128]{1,0:T(8,128)(2,1)}, bf16[1024,128]{1,0:T(8,128)(2,1)S(1)}, u32[]{:S(2)}) copy-start(bf16[1024,128]{1,0:T(8,128)(2,1)S(1)} %get-tuple-element.27) | copy-start | bytes 786436
  27.5 33.1 %copy-start.14 = (bf16[1024,128]{1,0:T(8,128)(2,1)}, bf16[1024,128]{1,0:T(8,128)(2,1)S(1)}, u32[]{:S(2)}) copy-start(bf16[1024,128]{1,0:T(8,128)(2,1)S(1)} %get-tuple-element.25) | copy-start | bytes 786436
  27.5 33.1 %copy-start.16 = (bf16[1024,128]{1,0:T(8,128)(2,1)}, bf16[1024,128]{1,0:T(8,128)(2,1)S(1)}, u32[]{:S(2)}) copy-start(bf16[1024,128]{1,0:T(8,128)(2,1)S(1)} %get-tuple-element.28) | copy-start | bytes 786436
  35.9 14.1 %all-to-all-start.1 = ((bf16[8,16,128]{2,1,0:T(8,128)(2,1)}), bf16[8,16,128]{2,1,0:T(8,128)(2,1)S(1)}, u32[]{:S(2)}, u32[]{:S(2)}) async-start(bf16[8,16,128]{2,1,0:T(8,128)(2,1)} %broadcast_in_dim.23), calls=%async_computation.1 | async-start | bytes 65536 | tf_op jit(solution)/shard_map/all_to_all | solution.py:52
  42.1 26.0 %copy-start.43 = (f32[256]{0:T(256)}, f32[256]{0:T(256)S(1)}, u32[]{:S(2)}) copy-start(f32[256]{0:T(256)S(1)} %add_convert_fusion.1) | copy-start | bytes 3076
  51.8 39.8 %copy-start.42 = (bf16[16,256]{1,0:T(8,128)(2,1)}, bf16[16,256]{1,0:T(8,128)(2,1)S(1)}, u32[]{:S(2)}) copy-start(bf16[16,256]{1,0:T(8,128)(2,1)S(1)} %get-tuple-element.50) | copy-start | bytes 24580
  52.5 15.6 %all-to-all-start.2 = ((bf16[64,4,128]{2,1,0:T(4,128)(2,1)}), bf16[64,4,128]{2,1,0:T(4,128)(2,1)S(1)}, u32[]{:S(2)}, u32[]{:S(2)}) async-start(bf16[64,4,128]{2,1,0:T(4,128)(2,1)} %broadcast_in_dim.24), calls=%async_computation.2 | async-start | bytes 131072 | tf_op jit(solution)/shard_map/all_to_all | solution.py:52
  59.4 3.1 %copy-start.34 = (f32[128]{0:T(128)}, f32[128]{0:T(128)S(1)}, u32[]{:S(2)}) copy-start(f32[128]{0:T(128)S(1)} %broadcast_multiply_fusion.7) | copy-start | bytes 1540
  60.6 8.4 %copy-start.45 = (f32[128]{0:T(128)}, f32[128]{0:T(128)S(1)}, u32[]{:S(2)}) copy-start(f32[128]{0:T(128)S(1)} %add_rsqrt_fusion.1) | copy-start | bytes 1540
  62.5 13.2 %copy-start.19 = (bf16[128,256]{1,0:T(8,128)(2,1)}, bf16[128,256]{1,0:T(8,128)(2,1)S(1)}, u32[]{:S(2)}) copy-start(bf16[128,256]{1,0:T(8,128)(2,1)S(1)} %get-tuple-element.41) | copy-start | bytes 196612
  68.1 7.6 %copy-start.8 = (bf16[64,4,128]{2,1,0:T(4,128)(2,1)}, bf16[64,4,128]{2,1,0:T(4,128)(2,1)S(1)}, u32[]{:S(2)}) copy-start(bf16[64,4,128]{2,1,0:T(4,128)(2,1)S(1)} %all-to-all-done.2) | copy-start | bytes 196612
  69.0 6.7 %copy-start.6 = (bf16[256,128]{1,0:T(8,128)(2,1)}, bf16[256,128]{1,0:T(8,128)(2,1)S(1)}, u32[]{:S(2)}) copy-start(bf16[256,128]{1,0:T(8,128)(2,1)S(1)} %get-tuple-element.55) | copy-start | bytes 196612
  69.8 20.6 %all-to-all-start.3 = ((f32[64,4,128]{2,1,0:T(4,128)}), f32[64,4,128]{2,1,0:T(4,128)}, u32[]{:S(2)}, u32[]{:S(2)}) async-start(f32[64,4,128]{2,1,0:T(4,128)} %bitcast.5), calls=%async_computation.3 | async-start | bytes 262144 | tf_op jit(solution)/shard_map/all_to_all | solution.py:52
  77.8 25.8 %copy-start.1 = (f32[512]{0:T(512)S(1)}, f32[512]{0:T(512)}, u32[]{:S(2)}) copy-start(f32[512]{0:T(512)} %param.17) | copy-start | bytes 6148
  92.4 11.2 %all-to-all-start.4 = ((bf16[8,16,128]{2,1,0:T(8,128)(2,1)}), bf16[8,16,128]{2,1,0:T(8,128)(2,1)S(1)}, u32[]{:S(2)}, u32[]{:S(2)}) async-start(bf16[8,16,128]{2,1,0:T(8,128)(2,1)} %broadcast_in_dim.26), calls=%async_computation.4 | async-start | bytes 65536 | tf_op jit(solution)/shard_map/all_to_all | solution.py:52
  112.1 14.8 %copy-start.5 = (bf16[128,1024]{1,0:T(8,128)(2,1)S(1)}, bf16[128,1024]{1,0:T(8,128)(2,1)}, u32[]{:S(2)}) copy-start(bf16[128,1024]{1,0:T(8,128)(2,1)} %param.13) | copy-start | bytes 786436
  112.1 14.9 %copy-start.29 = (f32[4]{0:T(128)S(1)}, f32[4]{0:T(128)}, u32[]{:S(2)}) copy-start(f32[4]{0:T(128)} %copy-done.28) | copy-start | bytes 52
  112.1 14.9 %copy-start.31 = (f32[4]{0:T(128)S(1)}, f32[4]{0:T(128)}, u32[]{:S(2)}) copy-start(f32[4]{0:T(128)} %copy-done.30) | copy-start | bytes 52
  112.8 12.8 %all-to-all-start.5 = ((f32[8,4,1152]{2,1,0:T(4,128)}), f32[8,4,1152]{2,1,0:T(4,128)S(1)}, u32[]{:S(2)}, u32[]{:S(2)}) async-start(f32[8,4,1152]{2,1,0:T(4,128)} %broadcast_in_dim.29), calls=%async_computation.5 | async-start | bytes 294912 | tf_op jit(solution)/shard_map/all_to_all | solution.py:52
  128.8 25.4 %copy-start.7 = (bf16[256,128]{1,0:T(8,128)(2,1)S(1)}, bf16[256,128]{1,0:T(8,128)(2,1)}, u32[]{:S(2)}) copy-start(bf16[256,128]{1,0:T(8,128)(2,1)} %copy-done.6) | copy-start | bytes 196612
  128.8 25.4 %copy-start.17 = (f32[128,256]{1,0:T(8,128)S(1)}, f32[128,256]{1,0:T(8,128)}, u32[]{:S(2)}) copy-start(f32[128,256]{1,0:T(8,128)} %get-tuple-element.40) | copy-start | bytes 393220
  128.8 25.6 %copy-start.20 = (bf16[128,256]{1,0:T(8,128)(2,1)S(1)}, bf16[128,256]{1,0:T(8,128)(2,1)}, u32[]{:S(2)}) copy-start(bf16[128,256]{1,0:T(8,128)(2,1)} %copy-done.19) | copy-start | bytes 196612
  128.8 25.6 %copy-start.38 = (s32[128]{0:T(128)S(1)}, s32[128]{0:T(128)}, u32[]{:S(2)}) copy-start(s32[128]{0:T(128)} %copy-done.37) | copy-start | bytes 1540
  128.9 25.6 %copy-start.44 = (f32[256]{0:T(256)S(1)}, f32[256]{0:T(256)}, u32[]{:S(2)}) copy-start(f32[256]{0:T(256)} %copy-done.43) | copy-start | bytes 3076
  128.9 25.6 %copy-start.48 = (f32[256,128]{1,0:T(8,128)S(1)}, f32[256,128]{1,0:T(8,128)}, u32[]{:S(2)}) copy-start(f32[256,128]{1,0:T(8,128)} %get-tuple-element.56) | copy-start | bytes 393220
  129.3 25.3 %copy-start.9 = (bf16[64,4,128]{2,1,0:T(4,128)(2,1)S(1)}, bf16[64,4,128]{2,1,0:T(4,128)(2,1)}, u32[]{:S(2)}) copy-start(bf16[64,4,128]{2,1,0:T(4,128)(2,1)} %copy-done.8) | copy-start | bytes 196612
  155.9 6.8 %copy-start.15 = (bf16[1024,128]{1,0:T(8,128)(2,1)S(1)}, bf16[1024,128]{1,0:T(8,128)(2,1)}, u32[]{:S(2)}) copy-start(bf16[1024,128]{1,0:T(8,128)(2,1)} %copy-done.14) | copy-start | bytes 786436
  156.8 25.8 %all-to-all-start.7 = ((bf16[64,36,128]{2,1,0:T(8,128)(2,1)}), bf16[64,36,128]{2,1,0:T(8,128)(2,1)S(1)}, u32[]{:S(2)}, u32[]{:S(2)}) async-start(bf16[64,36,128]{2,1,0:T(8,128)(2,1)} %pad_maximum_fusion), calls=%async_computation.8 | async-start | bytes 1310720 | tf_op jit(solution)/shard_map/all_to_all | solution.py:52
  162.7 51.3 %reduce-scatter.2.cloned.1.call-start = ((), (), s32[]{:S(2)}) async-start(), calls=%async_computation.12 | async-start | bytes 589824 | tf_op jit(solution)/shard_map/reduce_scatter | solution.py:275
  164.6 18.9 %copy-start.11 = (bf16[1024,128]{1,0:T(8,128)(2,1)S(1)}, bf16[1024,128]{1,0:T(8,128)(2,1)}, u32[]{:S(2)}) copy-start(bf16[1024,128]{1,0:T(8,128)(2,1)} %copy-done.10) | copy-start | bytes 786436
  164.6 18.9 %copy-start.13 = (bf16[1024,128]{1,0:T(8,128)(2,1)S(1)}, bf16[1024,128]{1,0:T(8,128)(2,1)}, u32[]{:S(2)}) copy-start(bf16[1024,128]{1,0:T(8,128)(2,1)} %copy-done.12) | copy-start | bytes 786436
  164.6 18.9 %copy-start.18 = (f32[16,1024]{1,0:T(8,128)S(1)}, f32[16,1024]{1,0:T(8,128)}, u32[]{:S(2)}) copy-start(f32[16,1024]{1,0:T(8,128)} %get-tuple-element.42) | copy-start | bytes 196612
  164.6 18.9 %copy-start.33 = (bf16[4,128]{1,0:T(4,128)(2,1)S(1)}, bf16[4,128]{1,0:T(4,128)(2,1)}, u32[]{:S(2)}) copy-start(bf16[4,128]{1,0:T(4,128)(2,1)} %copy-done.32) | copy-start | bytes 3076
  164.6 19.3 %copy-start.41 = (f32[16]{0:T(128)S(1)}, f32[16]{0:T(128)}, u32[]{:S(2)}) copy-start(f32[16]{0:T(128)} %copy-done.40) | copy-start | bytes 196
  165.5 48.5 %copy-start.25 = (s32[256]{0:T(256)S(1)}, s32[256]{0:T(256)}, u32[]{:S(2)}) copy-start(s32[256]{0:T(256)} %param.18) | copy-start | bytes 3076
  165.6 48.5 %copy-start.39 = (s32[128]{0:T(128)S(1)}, s32[128]{0:T(128)}, u32[]{:S(2)}) copy-start(s32[128]{0:T(128)} %copy-done.37) | copy-start | bytes 1540
  184.6 11.1 %all-to-all-start.8 = ((f32[8,4,128]{2,1,0:T(4,128)}), f32[8,4,128]{2,1,0:T(4,128)S(1)}, u32[]{:S(2)}, u32[]{:S(2)}) async-start(f32[8,4,128]{2,1,0:T(4,128)} %multiply_bitcast_fusion.1), calls=%async_computation.9 | async-start | bytes 32768 | tf_op jit(solution)/shard_map/all_to_all | solution.py:52
  196.4 16.7 %all-to-all-start.9 = ((bf16[64,8,128]{2,1,0:T(8,128)(2,1)}), bf16[64,8,128]{2,1,0:T(8,128)(2,1)S(1)}, u32[]{:S(2)}, u32[]{:S(2)}) async-start(bf16[64,8,128]{2,1,0:T(8,128)(2,1)} %broadcast_in_dim.32), calls=%async_computation.10 | async-start | bytes 262144 | tf_op jit(solution)/shard_map/all_to_all | solution.py:52
  (13 other events, 16.8 us)
Sparse Core Ops, SparseCore 0:
  10.1 38.5 all-gather.5
  50.9 38.8 all-gather.3
  166.3 37.0 reduce-scatter.1

commit v3 on v2

--- a/solution.py
+++ b/solution.py
@@ -56,48 +56,80 @@
     return swap(jnp.broadcast_to(block[None], (size,) + block.shape), axis)
 
 
+def select_kernel(first_ref, points_ref, history_ref, user_ref, picked_ref, joined_ref):
+    rows, requests = history_ref.shape[0], points_ref.shape[1]
+    positions = lax.broadcasted_iota(jnp.int32, (rows, requests), 0) + first_ref[0]
+    matches = jnp.where(positions == points_ref[...], 1.0, 0.0).astype(BF16)
+    picked = mm(matches, history_ref[...], ((0,), (0,)))
+    picked_ref[...] = picked.astype(BF16)
+    joined_ref[:, : history_ref.shape[1]] = history_ref[...]
+    joined_ref[:, history_ref.shape[1] :] = user_ref[...]
+
+
+def select_rows(first_row, points, history, user):
+    vmem = pl.BlockSpec(memory_space=pltpu.VMEM)
+    rows, width = history.shape
+    return pl.pallas_call(
+        select_kernel,
+        out_shape=(
+            jax.ShapeDtypeStruct((points.shape[0], width), BF16),
+            jax.ShapeDtypeStruct((rows, width + user.shape[1]), BF16),
+        ),
+        in_specs=[pl.BlockSpec(memory_space=pltpu.SMEM)] + [vmem] * 3,
+        out_specs=(vmem, vmem),
+    )(first_row[None], points[None], history, user)
+
+
 def score_kernel(
     count,
     request_ref,
     gated_ref,
     merge_ref,
     user_ref,
-    item_ref,
+    items_hbm,
     weight_ref,
     owner_ref,
-    row_ref,
     target_ref,
     cand_ref,
     out_ref,
     user_proj,
+    items_ref,
+    item_sems,
 ):
     heads = gated_ref.shape[0]
+    slots, hidden = owner_ref.shape[0], user_ref.shape[1]
+    item_copies = [
+        pltpu.make_async_copy(
+            items_hbm.at[pl.ds(request * slots, slots)],
+            items_ref.at[pl.ds(request * slots, slots)],
+            item_sems.at[request],
+        )
+        for request in range(count)
+    ]
+    for copy in item_copies:
+        copy.start()
     gated = jnp.concatenate([gated_ref[head] for head in range(heads)], 1)
     layer_out = request_ref[...].astype(F32) + mm(gated, merge_ref[...])
-    user_proj[...] = mm(layer_out.astype(BF16), user_ref[...])
-    slots, hidden = owner_ref.shape[0], user_ref.shape[1]
-    table_rows = item_ref.shape[0]
+    user_proj[...] = 0.5 * mm(layer_out.astype(BF16), user_ref[...])
     weights = weight_ref[...]
-    out_ref[...] = jnp.zeros_like(out_ref)
-    lanes = lax.broadcasted_iota(jnp.int32, (CHUNK, table_rows), 1)
     for request in range(count):
         user_row = user_proj[request : request + 1, :]
+        item_copies[request].wait()
 
         def step(index, sums, request=request, user_row=user_row):
             begin = pl.multiple_of(index * CHUNK, CHUNK)
             owned = owner_ref[pl.ds(begin, CHUNK), request : request + 1] == cand_ref[0]
-            place = row_ref[pl.ds(begin, CHUNK), request : request + 1]
             target = target_ref[pl.ds(begin, CHUNK), request : request + 1]
-            chosen = jnp.where(lanes == place, 1.0, 0.0).astype(BF16)
-            pre_score = mm(chosen, item_ref[...]) + user_row
-            part = 0.5 + 0.5 * jnp.tanh(0.5 * pre_score)
-            smooth = pre_score * part
-            slope = part + smooth * (1.0 - part)
+            items = items_ref[pl.ds(request * slots + begin, CHUNK), :]
+            half = items.astype(F32) + user_row
+            above = 1.0 + jnp.tanh(half)
+            smooth = half * above
+            slope = above * ((half + half + 1.0) - smooth)
             scores = jnp.sum(smooth * weights, -1, keepdims=True)
             power = jnp.where(owned, jnp.exp(scores), 0.0)
             target = jnp.where(owned, target, 0.0)
-            soft = (0.25 * power * slope).reshape(-1, 8, hidden)
-            hard = (target * slope).reshape(-1, 8, hidden)
+            soft = ((0.125 * power) * slope).reshape(-1, 8, hidden)
+            hard = ((0.5 * target) * slope).reshape(-1, 8, hidden)
             scalars = jnp.where(
                 lax.broadcasted_iota(jnp.int32, (CHUNK, HEAD), 1) == 0, power, target * scores
             )
@@ -116,20 +148,27 @@
         out_ref[request : request + 1, 2 * hidden :] = jnp.sum(sums[2], 0, keepdims=True)
 
 
-def score_parts(count, cand, request_rows, gated, merge, user, items, weights, owner, row, target):
+def score_parts(count, cand, request_rows, gated, merge, user, items, weights, owner, target):
     vmem = pl.BlockSpec(memory_space=pltpu.VMEM)
     hidden = user.shape[1]
     return pl.pallas_call(
         functools.partial(score_kernel, count),
-        out_shape=jax.ShapeDtypeStruct((8, 2 * hidden + HEAD), F32),
-        in_specs=[vmem] * 9 + [pl.BlockSpec(memory_space=pltpu.SMEM)],
+        out_shape=jax.ShapeDtypeStruct((count, 2 * hidden + HEAD), F32),
+        in_specs=[vmem] * 4
+        + [pl.BlockSpec(memory_space=pltpu.HBM)]
+        + [vmem] * 3
+        + [pl.BlockSpec(memory_space=pltpu.SMEM)],
         out_specs=vmem,
-        scratch_shapes=[pltpu.VMEM((PAD, hidden), F32)],
-        compiler_params=pltpu.CompilerParams(vmem_limit_bytes=48 * 1024 * 1024),
+        scratch_shapes=[
+            pltpu.VMEM((PAD, hidden), F32),
+            pltpu.VMEM(items.shape, BF16),
+            pltpu.SemaphoreType.DMA((count,)),
+        ],
+        compiler_params=pltpu.CompilerParams(vmem_limit_bytes=16 * 1024 * 1024),
         cost_estimate=pl.CostEstimate(
-            flops=3 * 10**9, bytes_accessed=5 * 10**6, transcendentals=10**6
+            flops=10**8, bytes_accessed=5 * 10**6, transcendentals=10**6
         ),
-    )(request_rows, gated, merge, user, items, weights, owner, row, target, cand)
+    )(request_rows, gated, merge, user, items, weights, owner, target, cand)
 
 
 def per_device(
@@ -158,14 +197,12 @@
     first_row = ctx * rows
     scaling = HEAD ** (-0.5)
 
-    riding = lax.all_gather(
-        jnp.concatenate([history, user_weights], 1), "cand", axis=0, tiled=False
-    )
+    picked, joined = select_rows(first_row, request_points, history, user_weights)
+    riding = lax.all_gather(joined, "cand", axis=0, tiled=False)
     merge_full = lax.all_gather(merge_weights, "cand", axis=0, tiled=True)
-
     positions = first_row + jnp.arange(rows, dtype=jnp.int32)
     matches = (request_points[:, None] == positions[None, :]).astype(BF16)
-    picked = mm(matches, history).astype(BF16).reshape(n_ctx, own, width)
+    picked = picked.reshape(n_ctx, own, width)
     picked = swap(picked, "ctx")
     picked = jnp.sum(picked.astype(F32), 0).astype(BF16)
 
@@ -199,15 +236,19 @@
     divisor = (request_points + 1).astype(F32)[:, None]
     logit_smooth, logit_slope = sigmoid_slope(logits)
     weight = jnp.where(allowed, logit_smooth / divisor, 0.0).astype(BF16)
-    attended = swap(mm(weight, values).reshape(n_ctx, own, HEAD), "ctx")
-    attended = jnp.sum(attended, 0)
+    attended = mm(weight, values).astype(BF16).reshape(n_ctx, own, HEAD)
+    candidate_row, attended = lax.optimization_barrier((candidate_row, attended))
+    attended = jnp.sum(swap(attended, "ctx").astype(F32), 0)
+    item_proj = (0.5 * mm(cand_table, item_weights)).astype(BF16)
+    lanes = jnp.arange(item_proj.shape[0], dtype=jnp.int32)
+    chosen = (candidate_row.reshape(-1)[:, None] == lanes[None, :]).astype(BF16)
+    items = mm(chosen, item_proj).astype(BF16)
     normed, inverse = layer_norm(attended)
     gated = (normed * gate).astype(BF16)
 
-    item_proj = mm(cand_table, item_weights).astype(BF16)
     target = (relevance + 1).astype(F32)
     target = target / jnp.sum(target, -1, keepdims=True)
-    gated, merge_full, user_full = lax.optimization_barrier((gated, merge_full, user_full))
+    gated, items = lax.optimization_barrier((gated, items))
     gated_full = send_all(jnp.pad(gated, ((0, PAD - own), (0, 0))), "cand", n_cand)
     parts = score_parts(
         own,
@@ -216,13 +257,12 @@
         gated_full,
         merge_full,
         user_full,
-        item_proj,
+        items,
         score_weights[None],
         candidate_owner.T,
-        candidate_row.T,
         target.T,
     )
-    parts = jnp.sum(send_all(parts[:own], "cand", n_cand).reshape(n_cand, own, -1), 0)
+    parts = jnp.sum(send_all(parts, "cand", n_cand).reshape(n_cand, own, -1), 0)
     total = parts[:, 2 * hidden : 2 * hidden + 1]
     losses = jnp.log(total[:, 0]) - parts[:, 2 * hidden + 1]
     d_user = parts[:, :hidden] / (0.25 * total) - parts[:, hidden : 2 * hidden]
@@ -233,24 +273,24 @@
     d_before_gate = (d_gated * normed * slope_request[:own, :HEAD]).astype(BF16)
 
     blocks = features // HEAD
-    strips = jnp.concatenate(
+
+    def strips_of(wide):
+        wide = wide.reshape(own, blocks, HEAD).transpose(1, 0, 2)
+        return jnp.repeat(wide, n_ctx // blocks, axis=0)
+
+    shared = jnp.concatenate([d_attended, gated, d_before_gate], 0)
+    sent = jnp.concatenate(
         [
-            request_low[:own].reshape(own, blocks, HEAD).transpose(1, 0, 2),
-            d_picked.astype(BF16).reshape(own, blocks, HEAD).transpose(1, 0, 2),
+            jnp.broadcast_to(shared[None], (n_ctx,) + shared.shape),
+            strips_of(d_picked.astype(BF16)),
         ],
         1,
-    )
-    strips = jnp.repeat(strips, n_ctx // blocks, axis=0)
-    shared = jnp.concatenate([d_attended, gated, d_before_gate], 0)
-    sent = jnp.concatenate(
-        [jnp.broadcast_to(shared[None], (n_ctx,) + shared.shape), strips], 1
     )
     sent = swap(sent, "ctx")
     all_grads = sent[:, :own].reshape(requests, HEAD)
     all_gated = sent[:, own : 2 * own].reshape(requests, HEAD)
     all_gate_grads = sent[:, 2 * own : 3 * own].reshape(requests, HEAD)
-    x_block = sent[:, 3 * own : 4 * own].reshape(requests, HEAD)
-    d_block = sent[:, 4 * own :].reshape(requests, HEAD)
+    d_block = sent[:, 3 * own :].reshape(requests, HEAD)
     lane = lax.rem(ctx, n_ctx // blocks) * strip
     grad_merge = mm(d_block, all_gated, ((0,), (0,)))
     grad_merge = lax.dynamic_slice_in_dim(grad_merge, lane, strip, 0).T
@@ -265,9 +305,17 @@
     dense_grad = mm(x_low, dense, ((0,), (0,))).astype(BF16)
     dense_grad = dense_grad.reshape(n_ctx, strip, 2 * HEAD)
     dense_grad = jnp.concatenate(
-        [dense_grad[:, :, :HEAD], dense_grad[:, :, HEAD:], d_query.reshape(n_ctx, own, HEAD)], 1
-    )
-    dense_grad = jnp.sum(swap(dense_grad, "ctx").astype(F32), 0)
+        [
+            dense_grad[:, :, :HEAD],
+            dense_grad[:, :, HEAD:],
+            d_query.reshape(n_ctx, own, HEAD),
+            strips_of(request_low[:own]),
+        ],
+        1,
+    )
+    dense_grad = swap(dense_grad, "ctx")
+    x_block = dense_grad[:, 2 * strip + own :].reshape(requests, HEAD)
+    dense_grad = jnp.sum(dense_grad[:, : 2 * strip + own].astype(F32), 0)
     own_query_grad = dense_grad[2 * strip :]
     d_before_query = (own_query_grad * slope_request[:own, HEAD:]).astype(BF16)
 

time: 224 us -> 206 us (0.920)
  blocking collectives: 24.7 us -> 12.3 us
  waiting for transfers between devices: 85.3 us -> 79.2 us
  other arithmetic: 12.6 us -> 8.73 us
  local copies, waits for them, and re-layouts: 9.48 us -> 13 us
  starting transfers between devices: 55.1 us -> 57.8 us
    all_to_all x1, blocking collectives: 24.7 us -> 12.3 us  [swap(): return lax.all_to_all(block, axis, 0, 0, tiled=True)]
    all_to_all x9, waiting for transfers between devices: 84.5 us -> 78.5 us  [swap(): return lax.all_to_all(block, axis, 0, 0, tiled=True)]
    unnamed x102 -> x90, local copies, waits for them, and re-layouts: 2.89 us -> 5.77 us
    all_to_all x9, starting transfers between devices: 55 us -> 57.7 us  [swap(): return lax.all_to_all(block, axis, 0, 0, tiled=True)]
    pallas_call x1, Pallas kernels: 6.85 us -> 4.18 us  [score_parts(): pl.pallas_call(functools.partial(score_kernel, count), out_shape=jax.Shap...]
    dot_general x18 -> x17, matrix products: 13.7 us -> 13.1 us  [mm(): lax.dot_general(left, right, (dims, ((), ())), preferred_element_type=F32)]
  transfers between devices with their start and end apart: 12 -> 12, of which waited for: 9 -> 9; matrix products, arithmetic and copies ran while one was open for 10% -> 11% of each run, Pallas kernels for 0% -> 0%
where the time goes in v3:
time: 206 us; the launch traced here: 205 us
  waiting for transfers between devices  79.2 us (38%)
  starting transfers between devices  57.8 us (28%)
  between operations  14.6 us (7%)
  matrix products  13.1 us (6%)
  local copies, waits for them, and re-layouts  13 us (6%)
  blocking collectives  12.3 us (6%)
  other arithmetic  8.73 us (4%)
  Pallas kernels  6.03 us (3%)
    all_to_all x9, waiting for transfers between devices, swap(): return lax.all_to_all(block, axis, 0, 0, tiled=True)  78.5 us
    all_to_all x9, starting transfers between devices, swap(): return lax.all_to_all(block, axis, 0, 0, tiled=True)  57.7 us
    dot_general x17, matrix products, mm(): lax.dot_general(left, right, (dims, ((), ())), preferred_element_type=F32)  13.1 us
    all_to_all x1, blocking collectives, swap(): return lax.all_to_all(block, axis, 0, 0, tiled=True)  12.3 us
    unnamed x90, local copies, waits for them, and re-layouts  5.77 us
    pallas_call x1, Pallas kernels, score_parts(): pl.pallas_call(functools.partial(score_kernel, count), out_shape=jax.Shap...  4.18 us
  transfers between devices with their start and end apart: 12, of which 9 were waited for; matrix products, arithmetic and copies ran while one was open for 11% of the time, Pallas kernels for 0%

profile of v3, /device:TPU:8, one launch (start us, length us, event | category | flops | bytes accessed | tf_op | source)
XLA Modules:
  0.0 204.9 jit_solution(12045634827548641424)
XLA Ops:
  7.2 1.9 shard_map.138
  9.1 14.8 %all-to-all-start = ((bf16[64,4,128]{2,1,0:T(4,128)(2,1)}), bf16[64,4,128]{2,1,0:T(4,128)(2,1)S(1)}, u32[]{:S(2)}, u32[]{:S(2)}) async-start(bf16[64,4,128]{2,1,0:T(4,128)(2,1)} %bitcast.131), calls=%async_computation | async-start | bytes 131072 | tf_op jit(solution)/shard_map/all_to_all | solution.py:52
  24.0 0.7 all-gather.4.cloned.1.call-update
  24.7 1.3 fusion.76
  26.6 7.2 %all-to-all-done = bf16[64,4,128]{2,1,0:T(4,128)(2,1)S(1)} async-done(((bf16[64,4,128]{2,1,0:T(4,128)(2,1)}), bf16[64,4,128]{2,1,0:T(4,128)(2,1)S(1)}, u32[]{:S(2)}, u32[]{:S(2)}) %all-to-all-start) | async-done | bytes 65568 | tf_op jit(solution)/shard_map/all_to_all | solution.py:52
  33.8 0.6 broadcast_in_dim.31
  34.5 6.2 %all-to-all-start.1 = ((bf16[8,16,128]{2,1,0:T(8,128)(2,1)}), bf16[8,16,128]{2,1,0:T(8,128)(2,1)S(1)}, u32[]{:S(2)}, u32[]{:S(2)}) async-start(bf16[8,16,128]{2,1,0:T(8,128)(2,1)} %broadcast_in_dim.31), calls=%async_computation.1 | async-start | bytes 65536 | tf_op jit(solution)/shard_map/all_to_all | solution.py:52
  40.7 7.8 %all-to-all-done.1 = bf16[8,16,128]{2,1,0:T(8,128)(2,1)S(1)} async-done(((bf16[8,16,128]{2,1,0:T(8,128)(2,1)}), bf16[8,16,128]{2,1,0:T(8,128)(2,1)S(1)}, u32[]{:S(2)}, u32[]{:S(2)}) %all-to-all-start.1) | async-done | bytes 32800 | tf_op jit(solution)/shard_map/all_to_all | solution.py:52
  49.4 0.6 broadcast_in_dim.32
  50.1 5.9 %all-to-all-start.2 = ((bf16[64,4,128]{2,1,0:T(4,128)(2,1)}), bf16[64,4,128]{2,1,0:T(4,128)(2,1)S(1)}, u32[]{:S(2)}, u32[]{:S(2)}) async-start(bf16[64,4,128]{2,1,0:T(4,128)(2,1)} %broadcast_in_dim.32), calls=%async_computation.2 | async-start | bytes 131072 | tf_op jit(solution)/shard_map/all_to_all | solution.py:52
  56.0 1.1 convert_reduce_fusion.1
  57.1 1.2 fusion.12
  58.8 1.3 add_multiply_fusion
  60.1 5.7 %all-to-all-done.2 = bf16[64,4,128]{2,1,0:T(4,128)(2,1)S(1)} async-done(((bf16[64,4,128]{2,1,0:T(4,128)(2,1)}), bf16[64,4,128]{2,1,0:T(4,128)(2,1)S(1)}, u32[]{:S(2)}, u32[]{:S(2)}) %all-to-all-start.2) | async-done | bytes 65568 | tf_op jit(solution)/shard_map/all_to_all | solution.py:52
  65.8 0.8 fusion.20
  66.6 0.8 convolution_convert_fusion.1
  67.4 5.6 %all-to-all-start.3 = ((bf16[64,4,128]{2,1,0:T(4,128)(2,1)}), bf16[64,4,128]{2,1,0:T(4,128)(2,1)S(1)}, u32[]{:S(2)}, u32[]{:S(2)}) async-start(bf16[64,4,128]{2,1,0:T(4,128)(2,1)} %bitcast.7), calls=%async_computation.3 | async-start | bytes 131072 | tf_op jit(solution)/shard_map/all_to_all | solution.py:52
  73.0 4.4 %fusion.1.items_hbm = bf16[2048,512]{1,0:T(8,128)(2,1)} fusion(s32[2048]{0:T(1024)S(1)} %bitcast.136, bf16[512,1024]{1,0:T(8,128)(2,1)S(1)} %copy-done, bf16[1024,512]{1,0:T(8,128)(2,1)} %param.16), kind=kOutput, calls=%fused_computation.2 | convolution fusion | flops 1613234176 | bytes 4202496 | tf_op jit(solution)/shard_map/dot_general | solution.py:38
  77.4 5.5 %all-to-all-done.3 = bf16[64,4,128]{2,1,0:T(4,128)(2,1)S(1)} async-done(((bf16[64,4,128]{2,1,0:T(4,128)(2,1)}), bf16[64,4,128]{2,1,0:T(4,128)(2,1)S(1)}, u32[]{:S(2)}, u32[]{:S(2)}) %all-to-all-start.3) | async-done | bytes 65568 | tf_op jit(solution)/shard_map/all_to_all | solution.py:52
  83.4 0.6 broadcast_in_dim.34
  84.0 4.7 %all-to-all-start.4 = ((bf16[8,16,128]{2,1,0:T(8,128)(2,1)}), bf16[8,16,128]{2,1,0:T(8,128)(2,1)S(1)}, u32[]{:S(2)}, u32[]{:S(2)}) async-start(bf16[8,16,128]{2,1,0:T(8,128)(2,1)} %broadcast_in_dim.34), calls=%async_computation.4 | async-start | bytes 65536 | tf_op jit(solution)/shard_map/all_to_all | solution.py:52
  88.8 1.3 slice.178
  90.0 6.6 %all-to-all-done.4.gated_ref = bf16[8,16,128]{2,1,0:T(8,128)(2,1)S(1)} async-done(((bf16[8,16,128]{2,1,0:T(8,128)(2,1)}), bf16[8,16,128]{2,1,0:T(8,128)(2,1)S(1)}, u32[]{:S(2)}, u32[]{:S(2)}) %all-to-all-start.4) | async-done | bytes 32800 | tf_op jit(solution)/shard_map/all_to_all | solution.py:52
  96.7 1.6 copy-done.1
  98.3 1.6 copy-done.2
  99.9 4.2 %shard_map.139 = f32[4,1152]{1,0:T(4,128)S(1)} custom-call(bf16[16,1024]{1,0:T(8,128)(2,1)S(1)} %copy_bitcast_fusion.request_ref, bf16[8,16,128]{2,1,0:T(8,128)(2,1)S(1)} %all-to-all-done.4.gated_ref, bf16[1024,1024]{1,0:T(8,128)(2,1)S(1)} %copy-done.1, bf16[1024,512]{1,0:T(8,128)(2,1)S(1)} %bitcast.105, bf16[2048,512]{1,0:T(8,128)(2,1)S(1)} %copy-done.2, ...), custom_call_target="tpu_custom_call" | custom-call | flops 100000000 | bytes 5000000 | tf_op jit(solution)/shard_map/pallas_call | solution.py:154
  104.1 12.3 %all_to_all.50 = f32[8,4,1152]{2,1,0:T(4,128)S(1)} all-to-all(f32[8,4,1152]{2,1,0:T(4,128)S(1)} %broadcast_in_dim.37), channel_id=1, replica_groups=mesh['ctx'=64,'cand'=8] {'cand'}, dimensions={0} | all-to-all | bytes 294912 | tf_op jit(solution)/shard_map/all_to_all | solution.py:52
  116.4 0.7 multiply_reduce_fusion.3
  118.2 0.6 copy-done.25
  118.8 0.8 pad_maximum_fusion.7
  119.7 5.5 %all-to-all-start.6 = ((bf16[64,16,128]{2,1,0:T(8,128)(2,1)}), bf16[64,16,128]{2,1,0:T(8,128)(2,1)S(1)}, u32[]{:S(2)}, u32[]{:S(2)}) async-start(bf16[64,16,128]{2,1,0:T(8,128)(2,1)} %pad_maximum_fusion.7), calls=%async_computation.6 | async-start | bytes 524288 | tf_op jit(solution)/shard_map/all_to_all | solution.py:52
  125.2 0.8 slice_bitcast_fusion
  126.1 11.6 %all-to-all-done.6 = bf16[64,16,128]{2,1,0:T(8,128)(2,1)S(1)} async-done(((bf16[64,16,128]{2,1,0:T(8,128)(2,1)}), bf16[64,16,128]{2,1,0:T(8,128)(2,1)S(1)}, u32[]{:S(2)}, u32[]{:S(2)}) %all-to-all-start.6) | async-done | bytes 262176 | tf_op jit(solution)/shard_map/all_to_all | solution.py:52
  139.2 1.0 pad_maximum_fusion
  140.2 5.2 %all-to-all-start.7 = ((bf16[64,40,128]{2,1,0:T(8,128)(2,1)}), bf16[64,40,128]{2,1,0:T(8,128)(2,1)S(1)}, u32[]{:S(2)}, u32[]{:S(2)}) async-start(bf16[64,40,128]{2,1,0:T(8,128)(2,1)} %pad_maximum_fusion), calls=%async_computation.8 | async-start | bytes 1310720 | tf_op jit(solution)/shard_map/all_to_all | solution.py:52
  145.5 1.4 fusion.71
  147.3 0.9 copy.107
  148.3 16.8 %all-to-all-done.7 = bf16[64,40,128]{2,1,0:T(8,128)(2,1)S(1)} async-done(((bf16[64,40,128]{2,1,0:T(8,128)(2,1)}), bf16[64,40,128]{2,1,0:T(8,128)(2,1)S(1)}, u32[]{:S(2)}, u32[]{:S(2)}) %all-to-all-start.7) | async-done | bytes 655392 | tf_op jit(solution)/shard_map/all_to_all | solution.py:52
  165.2 0.7 fusion.52
  166.3 0.7 multiply_bitcast_fusion.1
  167.0 3.3 %all-to-all-start.8 = ((f32[8,4,128]{2,1,0:T(4,128)}), f32[8,4,128]{2,1,0:T(4,128)S(1)}, u32[]{:S(2)}, u32[]{:S(2)}) async-start(f32[8,4,128]{2,1,0:T(4,128)} %multiply_bitcast_fusion.1), calls=%async_computation.9 | async-start | bytes 32768 | tf_op jit(solution)/shard_map/all_to_all | solution.py:52
  170.6 7.5 %all-to-all-done.8 = f32[8,4,128]{2,1,0:T(4,128)S(1)} async-done(((f32[8,4,128]{2,1,0:T(4,128)}), f32[8,4,128]{2,1,0:T(4,128)S(1)}, u32[]{:S(2)}, u32[]{:S(2)}) %all-to-all-start.8) | async-done | bytes 16416 | tf_op jit(solution)/shard_map/all_to_all | solution.py:52
  178.1 0.7 broadcast_in_dim.41
  178.8 6.5 %all-to-all-start.9 = ((bf16[64,8,128]{2,1,0:T(8,128)(2,1)}), bf16[64,8,128]{2,1,0:T(8,128)(2,1)S(1)}, u32[]{:S(2)}, u32[]{:S(2)}) async-start(bf16[64,8,128]{2,1,0:T(8,128)(2,1)} %broadcast_in_dim.41), calls=%async_computation.10 | async-start | bytes 262144 | tf_op jit(solution)/shard_map/all_to_all | solution.py:52
  185.3 0.6 dynamic-slice_bitcast_fusion
  186.0 9.7 %all-to-all-done.9 = bf16[64,8,128]{2,1,0:T(8,128)(2,1)S(1)} async-done(((bf16[64,8,128]{2,1,0:T(8,128)(2,1)}), bf16[64,8,128]{2,1,0:T(8,128)(2,1)S(1)}, u32[]{:S(2)}, u32[]{:S(2)}) %all-to-all-start.9) | async-done | bytes 131104 | tf_op jit(solution)/shard_map/all_to_all | solution.py:52
  196.0 0.6 pad_maximum_fusion.11
  196.6 1.8 convolution_add_fusion
  (157 shorter events, 6.6 us)
Async XLA Ops:
  7.2 65.8 %copy-start = (bf16[512,1024]{1,0:T(8,128)(2,1)S(1)}, bf16[512,1024]{1,0:T(8,128)(2,1)}, u32[]{:S(2)}) copy-start(bf16[512,1024]{1,0:T(8,128)(2,1)} %param.14) | copy-start | bytes 3145732
  7.2 48.8 %all-gather.6.cloned.1.call-start = ((), (), s32[]{:S(2)}) async-start(), calls=%async_computation.13 | async-start | bytes 1474560 | tf_op jit(solution)/shard_map/all_gather | solution.py:201
  9.1 17.0 %copy-start.19 = (s32[4,512]{1,0:T(4,128)S(1)}, s32[4,512]{1,0:T(4,128)}, u32[]{:S(2)}) copy-start(s32[4,512]{1,0:T(4,128)} %param.21) | copy-start | bytes 24580
  9.1 24.6 %all-to-all-start = ((bf16[64,4,128]{2,1,0:T(4,128)(2,1)}), bf16[64,4,128]{2,1,0:T(4,128)(2,1)S(1)}, u32[]{:S(2)}, u32[]{:S(2)}) async-start(bf16[64,4,128]{2,1,0:T(4,128)(2,1)} %bitcast.131), calls=%async_computation | async-start | bytes 131072 | tf_op jit(solution)/shard_map/all_to_all | solution.py:52
  23.9 2.5 %copy-start.23 = (s32[4,512]{1,0:T(4,128)S(1)}, s32[4,512]{1,0:T(4,128)}, u32[]{:S(2)}) copy-start(s32[4,512]{1,0:T(4,128)} %param.19) | copy-start | bytes 24580
  23.9 72.7 %all-gather.4.cloned.1.call-start = ((), (), s32[]{:S(2)}) async-start(), calls=%async_computation.11 | async-start | bytes 2359296 | tf_op jit(solution)/shard_map/all_gather | solution.py:202
  24.7 1.9 copy-start.20
  26.0 34.0 %copy-start.6 = (bf16[1024,128]{1,0:T(8,128)(2,1)}, bf16[1024,128]{1,0:T(8,128)(2,1)S(1)}, u32[]{:S(2)}) copy-start(bf16[1024,128]{1,0:T(8,128)(2,1)S(1)} %get-tuple-element.32) | copy-start | bytes 786436
  26.0 34.0 %copy-start.8 = (bf16[1024,128]{1,0:T(8,128)(2,1)}, bf16[1024,128]{1,0:T(8,128)(2,1)S(1)}, u32[]{:S(2)}) copy-start(bf16[1024,128]{1,0:T(8,128)(2,1)S(1)} %get-tuple-element.33) | copy-start | bytes 786436
  26.0 34.0 %copy-start.10 = (bf16[1024,128]{1,0:T(8,128)(2,1)}, bf16[1024,128]{1,0:T(8,128)(2,1)S(1)}, u32[]{:S(2)}) copy-start(bf16[1024,128]{1,0:T(8,128)(2,1)S(1)} %get-tuple-element.31) | copy-start | bytes 786436
  26.0 34.0 %copy-start.11 = (bf16[1024,128]{1,0:T(8,128)(2,1)}, bf16[1024,128]{1,0:T(8,128)(2,1)S(1)}, u32[]{:S(2)}) copy-start(bf16[1024,128]{1,0:T(8,128)(2,1)S(1)} %get-tuple-element.34) | copy-start | bytes 786436
  26.6 39.2 %copy-start.32 = (f32[256]{0:T(256)}, f32[256]{0:T(256)S(1)}, u32[]{:S(2)}) copy-start(f32[256]{0:T(256)S(1)} %add_convert_fusion.1) | copy-start | bytes 3076
  34.5 14.1 %all-to-all-start.1 = ((bf16[8,16,128]{2,1,0:T(8,128)(2,1)}), bf16[8,16,128]{2,1,0:T(8,128)(2,1)S(1)}, u32[]{:S(2)}, u32[]{:S(2)}) async-start(bf16[8,16,128]{2,1,0:T(8,128)(2,1)} %broadcast_in_dim.31), calls=%async_computation.1 | async-start | bytes 65536 | tf_op jit(solution)/shard_map/all_to_all | solution.py:52
  40.7 25.1 %copy-start.38 = (s32[128]{0:T(128)}, s32[128]{0:T(128)S(1)}, u32[]{:S(2)}) copy-start(s32[128]{0:T(128)S(1)} %iota_add_fusion) | copy-start | bytes 1540
  48.9 11.1 %copy-start.14 = (bf16[16,1024]{1,0:T(8,128)(2,1)}, bf16[16,1024]{1,0:T(8,128)(2,1)S(1)}, u32[]{:S(2)}) copy-start(bf16[16,1024]{1,0:T(8,128)(2,1)S(1)} %get-tuple-element.48) | copy-start | bytes 98308
  49.4 68.7 %copy-start.34 = (f32[16,256]{1,0:T(8,128)}, f32[16,256]{1,0:T(8,128)S(1)}, u32[]{:S(2)}) copy-start(f32[16,256]{1,0:T(8,128)S(1)} %get-tuple-element.54) | copy-start | bytes 49156
  50.1 15.7 %all-to-all-start.2 = ((bf16[64,4,128]{2,1,0:T(4,128)(2,1)}), bf16[64,4,128]{2,1,0:T(4,128)(2,1)S(1)}, u32[]{:S(2)}, u32[]{:S(2)}) async-start(bf16[64,4,128]{2,1,0:T(4,128)(2,1)} %broadcast_in_dim.32), calls=%async_computation.2 | async-start | bytes 131072 | tf_op jit(solution)/shard_map/all_to_all | solution.py:52
  60.1 17.4 %copy-start.12 = (bf16[128,256]{1,0:T(8,128)(2,1)}, bf16[128,256]{1,0:T(8,128)(2,1)S(1)}, u32[]{:S(2)}) copy-start(bf16[128,256]{1,0:T(8,128)(2,1)S(1)} %get-tuple-element.46) | copy-start | bytes 196612
  60.1 12.9 %copy-start.24 = (s32[4,512]{1,0:T(4,128)S(1)}, s32[4,512]{1,0:T(4,128)}, u32[]{:S(2)}) copy-start(s32[4,512]{1,0:T(4,128)} %param.20) | copy-start | bytes 24580
  67.4 15.5 %all-to-all-start.3 = ((bf16[64,4,128]{2,1,0:T(4,128)(2,1)}), bf16[64,4,128]{2,1,0:T(4,128)(2,1)S(1)}, u32[]{:S(2)}, u32[]{:S(2)}) async-start(bf16[64,4,128]{2,1,0:T(4,128)(2,1)} %bitcast.7), calls=%async_computation.3 | async-start | bytes 131072 | tf_op jit(solution)/shard_map/all_to_all | solution.py:52
  77.4 19.3 %copy-start.3 = (f32[512]{0:T(512)S(1)}, f32[512]{0:T(512)}, u32[]{:S(2)}) copy-start(f32[512]{0:T(512)} %param.17) | copy-start | bytes 6148
  84.0 12.7 %all-to-all-start.4 = ((bf16[8,16,128]{2,1,0:T(8,128)(2,1)}), bf16[8,16,128]{2,1,0:T(8,128)(2,1)S(1)}, u32[]{:S(2)}, u32[]{:S(2)}) async-start(bf16[8,16,128]{2,1,0:T(8,128)(2,1)} %broadcast_in_dim.34), calls=%async_computation.4 | async-start | bytes 65536 | tf_op jit(solution)/shard_map/all_to_all | solution.py:52
  96.7 1.6 copy-start.1
  98.3 1.6 copy-start.2
  104.1 13.6 %copy-start.5 = (bf16[128,1024]{1,0:T(8,128)(2,1)S(1)}, bf16[128,1024]{1,0:T(8,128)(2,1)}, u32[]{:S(2)}) copy-start(bf16[128,1024]{1,0:T(8,128)(2,1)} %param.13) | copy-start | bytes 786436
  117.6 20.4 %copy-start.13 = (bf16[128,256]{1,0:T(8,128)(2,1)S(1)}, bf16[128,256]{1,0:T(8,128)(2,1)}, u32[]{:S(2)}) copy-start(bf16[128,256]{1,0:T(8,128)(2,1)} %copy-done.12) | copy-start | bytes 196612
  117.7 20.4 %copy-start.21 = (s32[256]{0:T(256)S(1)}, s32[256]{0:T(256)}, u32[]{:S(2)}) copy-start(s32[256]{0:T(256)} %param.18) | copy-start | bytes 3076
  117.7 20.4 %copy-start.33 = (f32[256]{0:T(256)S(1)}, f32[256]{0:T(256)}, u32[]{:S(2)}) copy-start(f32[256]{0:T(256)} %copy-done.32) | copy-start | bytes 3076
  117.7 20.4 %copy-start.39 = (s32[128]{0:T(128)S(1)}, s32[128]{0:T(128)}, u32[]{:S(2)}) copy-start(s32[128]{0:T(128)} %copy-done.38) | copy-start | bytes 1540
  117.7 20.4 %copy-start.41 = (f32[256,128]{1,0:T(8,128)S(1)}, f32[256,128]{1,0:T(8,128)}, u32[]{:S(2)}) copy-start(f32[256,128]{1,0:T(8,128)} %get-tuple-element.61) | copy-start | bytes 393220
  119.7 18.0 %all-to-all-start.6 = ((bf16[64,16,128]{2,1,0:T(8,128)(2,1)}), bf16[64,16,128]{2,1,0:T(8,128)(2,1)S(1)}, u32[]{:S(2)}, u32[]{:S(2)}) async-start(bf16[64,16,128]{2,1,0:T(8,128)(2,1)} %pad_maximum_fusion.7), calls=%async_computation.6 | async-start | bytes 524288 | tf_op jit(solution)/shard_map/all_to_all | solution.py:52
  125.2 13.4 %copy-start.4 = (bf16[1024,640]{1,0:T(8,128)(2,1)S(1)}, bf16[1024,640]{1,0:T(8,128)(2,1)}, u32[]{:S(2)}) copy-start(bf16[1024,640]{1,0:T(8,128)(2,1)} %all-gather.6.cloned.1.call-done) | copy-start | bytes 3932164
  125.2 13.4 %copy-start.28 = (f32[128]{0:T(128)S(1)}, f32[128]{0:T(128)}, u32[]{:S(2)}) copy-start(f32[128]{0:T(128)} %copy-done.27) | copy-start | bytes 1540
  125.2 13.4 %copy-start.36 = (f32[128]{0:T(128)S(1)}, f32[128]{0:T(128)}, u32[]{:S(2)}) copy-start(f32[128]{0:T(128)} %copy-done.35) | copy-start | bytes 1540
  139.2 6.3 %copy-start.16 = (bf16[128,128]{1,0:T(8,128)(2,1)S(1)}, bf16[128,128]{1,0:T(8,128)(2,1)}, u32[]{:S(2)}) copy-start(bf16[128,128]{1,0:T(8,128)(2,1)} %copy-done.15) | copy-start | bytes 98308
  139.2 6.3 %copy-start.18 = (bf16[128,128]{1,0:T(8,128)(2,1)S(1)}, bf16[128,128]{1,0:T(8,128)(2,1)}, u32[]{:S(2)}) copy-start(bf16[128,128]{1,0:T(8,128)(2,1)} %copy-done.17) | copy-start | bytes 98308
  139.2 6.3 %copy-start.29 = (f32[128]{0:T(128)S(1)}, f32[128]{0:T(128)}, u32[]{:S(2)}) copy-start(f32[128]{0:T(128)} %copy-done.27) | copy-start | bytes 1540
  139.2 6.3 %copy-start.37 = (f32[128]{0:T(128)S(1)}, f32[128]{0:T(128)}, u32[]{:S(2)}) copy-start(f32[128]{0:T(128)} %copy-done.35) | copy-start | bytes 1540
  140.2 24.8 %all-to-all-start.7 = ((bf16[64,40,128]{2,1,0:T(8,128)(2,1)}), bf16[64,40,128]{2,1,0:T(8,128)(2,1)S(1)}, u32[]{:S(2)}, u32[]{:S(2)}) async-start(bf16[64,40,128]{2,1,0:T(8,128)(2,1)} %pad_maximum_fusion), calls=%async_computation.8 | async-start | bytes 1310720 | tf_op jit(solution)/shard_map/all_to_all | solution.py:52
  145.4 51.2 %reduce-scatter.2.cloned.1.call-start = ((), (), s32[]{:S(2)}) async-start(), calls=%async_computation.12 | async-start | bytes 589824 | tf_op jit(solution)/shard_map/reduce_scatter | solution.py:323
  147.3 18.6 %copy-start.7 = (bf16[1024,128]{1,0:T(8,128)(2,1)S(1)}, bf16[1024,128]{1,0:T(8,128)(2,1)}, u32[]{:S(2)}) copy-start(bf16[1024,128]{1,0:T(8,128)(2,1)} %copy-done.6) | copy-start | bytes 786436
  147.3 18.6 %copy-start.9 = (bf16[1024,128]{1,0:T(8,128)(2,1)S(1)}, bf16[1024,128]{1,0:T(8,128)(2,1)}, u32[]{:S(2)}) copy-start(bf16[1024,128]{1,0:T(8,128)(2,1)} %copy-done.8) | copy-start | bytes 786436
  147.3 18.6 %copy-start.26 = (bf16[4,128]{1,0:T(4,128)(2,1)S(1)}, bf16[4,128]{1,0:T(4,128)(2,1)}, u32[]{:S(2)}) copy-start(bf16[4,128]{1,0:T(4,128)(2,1)} %copy-done.25) | copy-start | bytes 3076
  147.3 19.0 %copy-start.31 = (f32[16]{0:T(128)S(1)}, f32[16]{0:T(128)}, u32[]{:S(2)}) copy-start(f32[16]{0:T(128)} %copy-done.30) | copy-start | bytes 196
  165.2 31.4 %copy-start.22 = (s32[256]{0:T(256)S(1)}, s32[256]{0:T(256)}, u32[]{:S(2)}) copy-start(s32[256]{0:T(256)} %param.18) | copy-start | bytes 3076
  165.2 31.4 %copy-start.40 = (s32[128]{0:T(128)S(1)}, s32[128]{0:T(128)}, u32[]{:S(2)}) copy-start(s32[128]{0:T(128)} %copy-done.38) | copy-start | bytes 1540
  167.0 11.1 %all-to-all-start.8 = ((f32[8,4,128]{2,1,0:T(4,128)}), f32[8,4,128]{2,1,0:T(4,128)S(1)}, u32[]{:S(2)}, u32[]{:S(2)}) async-start(f32[8,4,128]{2,1,0:T(4,128)} %multiply_bitcast_fusion.1), calls=%async_computation.9 | async-start | bytes 32768 | tf_op jit(solution)/shard_map/all_to_all | solution.py:52
  178.8 16.9 %all-to-all-start.9 = ((bf16[64,8,128]{2,1,0:T(8,128)(2,1)}), bf16[64,8,128]{2,1,0:T(8,128)(2,1)S(1)}, u32[]{:S(2)}, u32[]{:S(2)}) async-start(bf16[64,8,128]{2,1,0:T(8,128)(2,1)} %broadcast_in_dim.41), calls=%async_computation.10 | async-start | bytes 262144 | tf_op jit(solution)/shard_map/all_to_all | solution.py:52
  (6 other events, 4.5 us)
Sparse Core Ops, SparseCore 0:
  10.1 37.2 all-gather.5
  49.5 38.1 all-gather.3
  149.0 36.1 reduce-scatter.1

commit v4 on v3

--- a/solution.py
+++ b/solution.py
@@ -12,7 +12,8 @@
 F32 = jnp.float32
 BF16 = jnp.bfloat16
 PAD = 16
-CHUNK = 128
+CHUNK = 64
+UNROLL = 8
 
 
 def sigmoid_slope(argument):
@@ -141,7 +142,7 @@
 
         zero = jnp.zeros((8, hidden), F32)
         sums = lax.fori_loop(
-            0, slots // CHUNK, step, (zero, zero, jnp.zeros((8, HEAD), F32)), unroll=2
+            0, slots // CHUNK, step, (zero, zero, jnp.zeros((8, HEAD), F32)), unroll=UNROLL
         )
         out_ref[request : request + 1, :hidden] = jnp.sum(sums[0], 0, keepdims=True)
         out_ref[request : request + 1, hidden : 2 * hidden] = jnp.sum(sums[1], 0, keepdims=True)
@@ -203,11 +204,13 @@
     positions = first_row + jnp.arange(rows, dtype=jnp.int32)
     matches = (request_points[:, None] == positions[None, :]).astype(BF16)
     picked = picked.reshape(n_ctx, own, width)
+    late_table, picked = lax.optimization_barrier((cand_table, picked))
+    item_proj = (0.5 * mm(late_table, item_weights)).astype(BF16)
     picked = swap(picked, "ctx")
     picked = jnp.sum(picked.astype(F32), 0).astype(BF16)
-
-    picked = send_all(jnp.pad(picked, ((0, PAD - own), (0, 0))), "cand", n_cand)
-    picked = picked.transpose(1, 0, 2).reshape(PAD, features)
+    picked, item_proj = lax.optimization_barrier((picked, item_proj))
+
+    picked = send_all(picked, "cand", n_cand).transpose(1, 0, 2).reshape(own, features)
     r_normed, r_inverse = layer_norm(picked.astype(F32))
     request_low = r_normed.astype(BF16)
     weights_request = jnp.concatenate(
@@ -239,7 +242,6 @@
     attended = mm(weight, values).astype(BF16).reshape(n_ctx, own, HEAD)
     candidate_row, attended = lax.optimization_barrier((candidate_row, attended))
     attended = jnp.sum(swap(attended, "ctx").astype(F32), 0)
-    item_proj = (0.5 * mm(cand_table, item_weights)).astype(BF16)
     lanes = jnp.arange(item_proj.shape[0], dtype=jnp.int32)
     chosen = (candidate_row.reshape(-1)[:, None] == lanes[None, :]).astype(BF16)
     items = mm(chosen, item_proj).astype(BF16)
@@ -248,12 +250,12 @@
 
     target = (relevance + 1).astype(F32)
     target = target / jnp.sum(target, -1, keepdims=True)
-    gated, items = lax.optimization_barrier((gated, items))
+    gated, items, user_full = lax.optimization_barrier((gated, items, user_full))
     gated_full = send_all(jnp.pad(gated, ((0, PAD - own), (0, 0))), "cand", n_cand)
     parts = score_parts(
         own,
         cand[None],
-        picked,
+        jnp.pad(picked, ((0, PAD - own), (0, 0))),
         gated_full,
         merge_full,
         user_full,

time: 206 us -> 205 us (level)
  waiting for transfers between devices: 79.2 us -> 82.8 us
  local copies, waits for them, and re-layouts: 13 us -> 9.6 us
    all_to_all x9, waiting for transfers between devices: 78.5 us -> 82.1 us  [swap(): return lax.all_to_all(block, axis, 0, 0, tiled=True)]
    unnamed x90 -> x68, local copies, waits for them, and re-layouts: 5.77 us -> 3.59 us
    dot_general x17 -> x18, matrix products: 13.1 us -> 12.8 us  [mm(): lax.dot_general(left, right, (dims, ((), ())), preferred_element_type=F32)]
  transfers between devices with their start and end apart: 12 -> 12, of which waited for: 9 -> 9; matrix products, arithmetic and copies ran while one was open for 11% -> 10% of each run, Pallas kernels for 0% -> 0%
where the time goes in v4:
time: 205 us; the launch traced here: 204 us
  waiting for transfers between devices  82.8 us (40%)
  starting transfers between devices  57.9 us (28%)
  between operations  14.5 us (7%)
  matrix products  12.8 us (6%)
  blocking collectives  12.8 us (6%)
  local copies, waits for them, and re-layouts  9.6 us (5%)
  other arithmetic  8.02 us (4%)
  Pallas kernels  5.59 us (3%)
    all_to_all x9, waiting for transfers between devices, swap(): return lax.all_to_all(block, axis, 0, 0, tiled=True)  82.1 us
    all_to_all x9, starting transfers between devices, swap(): return lax.all_to_all(block, axis, 0, 0, tiled=True)  57.8 us
    dot_general x18, matrix products, mm(): lax.dot_general(left, right, (dims, ((), ())), preferred_element_type=F32)  12.8 us
    all_to_all x1, blocking collectives, swap(): return lax.all_to_all(block, axis, 0, 0, tiled=True)  12.8 us
  transfers between devices with their start and end apart: 12, of which 9 were waited for; matrix products, arithmetic and copies ran while one was open for 10% of the time, Pallas kernels for 0%

profile of v4, /device:TPU:8, one launch (start us, length us, event | category | flops | bytes accessed | tf_op | source)
XLA Modules:
  0.0 204.0 jit_solution(17229112983591520063)
XLA Ops:
  7.2 1.9 shard_map.138
  9.1 15.0 %all-to-all-start = ((bf16[64,4,128]{2,1,0:T(4,128)(2,1)}), bf16[64,4,128]{2,1,0:T(4,128)(2,1)S(1)}, u32[]{:S(2)}, u32[]{:S(2)}) async-start(bf16[64,4,128]{2,1,0:T(4,128)(2,1)} %bitcast.122), calls=%async_computation | async-start | bytes 131072 | tf_op jit(solution)/shard_map/all_to_all | solution.py:53
  24.1 0.7 all-gather.4.cloned.1.call-update
  24.8 1.3 fusion.78
  26.2 1.5 fusion.3
  27.9 6.0 %all-to-all-done = bf16[64,4,128]{2,1,0:T(4,128)(2,1)S(1)} async-done(((bf16[64,4,128]{2,1,0:T(4,128)(2,1)}), bf16[64,4,128]{2,1,0:T(4,128)(2,1)S(1)}, u32[]{:S(2)}, u32[]{:S(2)}) %all-to-all-start) | async-done | bytes 65568 | tf_op jit(solution)/shard_map/all_to_all | solution.py:53
  34.0 0.6 broadcast_in_dim.31
  34.6 6.2 %all-to-all-start.1 = ((bf16[8,4,128]{2,1,0:T(4,128)(2,1)}), bf16[8,4,128]{2,1,0:T(4,128)(2,1)S(1)}, u32[]{:S(2)}, u32[]{:S(2)}) async-start(bf16[8,4,128]{2,1,0:T(4,128)(2,1)} %broadcast_in_dim.31), calls=%async_computation.1 | async-start | bytes 16384 | tf_op jit(solution)/shard_map/all_to_all | solution.py:53
  40.8 7.7 %all-to-all-done.1 = bf16[8,4,128]{2,1,0:T(4,128)(2,1)S(1)} async-done(((bf16[8,4,128]{2,1,0:T(4,128)(2,1)}), bf16[8,4,128]{2,1,0:T(4,128)(2,1)S(1)}, u32[]{:S(2)}, u32[]{:S(2)}) %all-to-all-start.1) | async-done | bytes 8224 | tf_op jit(solution)/shard_map/all_to_all | solution.py:53
  49.1 0.6 broadcast_in_dim.32
  49.7 5.2 %all-to-all-start.2 = ((bf16[64,4,128]{2,1,0:T(4,128)(2,1)}), bf16[64,4,128]{2,1,0:T(4,128)(2,1)S(1)}, u32[]{:S(2)}, u32[]{:S(2)}) async-start(bf16[64,4,128]{2,1,0:T(4,128)(2,1)} %broadcast_in_dim.32), calls=%async_computation.2 | async-start | bytes 131072 | tf_op jit(solution)/shard_map/all_to_all | solution.py:53
  55.0 1.1 convert_reduce_fusion.1
  56.1 1.2 fusion.12
  57.3 1.3 add_multiply_fusion
  58.6 6.2 %all-to-all-done.2 = bf16[64,4,128]{2,1,0:T(4,128)(2,1)S(1)} async-done(((bf16[64,4,128]{2,1,0:T(4,128)(2,1)}), bf16[64,4,128]{2,1,0:T(4,128)(2,1)S(1)}, u32[]{:S(2)}, u32[]{:S(2)}) %all-to-all-start.2) | async-done | bytes 65568 | tf_op jit(solution)/shard_map/all_to_all | solution.py:53
  64.8 0.8 fusion.19
  65.6 0.8 convolution_convert_fusion.1
  66.4 5.2 %all-to-all-start.3 = ((bf16[64,4,128]{2,1,0:T(4,128)(2,1)}), bf16[64,4,128]{2,1,0:T(4,128)(2,1)S(1)}, u32[]{:S(2)}, u32[]{:S(2)}) async-start(bf16[64,4,128]{2,1,0:T(4,128)(2,1)} %bitcast.9), calls=%async_computation.3 | async-start | bytes 131072 | tf_op jit(solution)/shard_map/all_to_all | solution.py:53
  71.6 2.6 %fusion.1.items_hbm = bf16[2048,512]{1,0:T(8,128)(2,1)} fusion(bf16[512,512]{1,0:T(8,128)(2,1)S(1)} %copy-done.30, s32[2048]{0:T(1024)S(1)} %bitcast.126), kind=kOutput, calls=%fused_computation.2 | convolution fusion | flops 1075838976 | bytes 2629632 | tf_op jit(solution)/shard_map/dot_general | solution.py:39
  74.3 7.7 %all-to-all-done.3 = bf16[64,4,128]{2,1,0:T(4,128)(2,1)S(1)} async-done(((bf16[64,4,128]{2,1,0:T(4,128)(2,1)}), bf16[64,4,128]{2,1,0:T(4,128)(2,1)S(1)}, u32[]{:S(2)}, u32[]{:S(2)}) %all-to-all-start.3) | async-done | bytes 65568 | tf_op jit(solution)/shard_map/all_to_all | solution.py:53
  82.5 0.6 broadcast_in_dim.34
  83.1 3.7 %all-to-all-start.4 = ((bf16[8,16,128]{2,1,0:T(8,128)(2,1)}), bf16[8,16,128]{2,1,0:T(8,128)(2,1)S(1)}, u32[]{:S(2)}, u32[]{:S(2)}) async-start(bf16[8,16,128]{2,1,0:T(8,128)(2,1)} %broadcast_in_dim.34), calls=%async_computation.4 | async-start | bytes 65536 | tf_op jit(solution)/shard_map/all_to_all | solution.py:53
  87.2 7.6 %all-to-all-done.4.gated_ref = bf16[8,16,128]{2,1,0:T(8,128)(2,1)S(1)} async-done(((bf16[8,16,128]{2,1,0:T(8,128)(2,1)}), bf16[8,16,128]{2,1,0:T(8,128)(2,1)S(1)}, u32[]{:S(2)}, u32[]{:S(2)}) %all-to-all-start.4) | async-done | bytes 32800 | tf_op jit(solution)/shard_map/all_to_all | solution.py:53
  94.8 1.6 copy-done.1
  96.4 1.6 copy-done.2
  98.0 3.7 %shard_map.139 = f32[4,1152]{1,0:T(4,128)S(1)} custom-call(bf16[16,1024]{1,0:T(8,128)(2,1)S(1)} %pad.8.request_ref, bf16[8,16,128]{2,1,0:T(8,128)(2,1)S(1)} %all-to-all-done.4.gated_ref, bf16[1024,1024]{1,0:T(8,128)(2,1)S(1)} %copy-done.1, bf16[1024,512]{1,0:T(8,128)(2,1)S(1)} %bitcast.95, bf16[2048,512]{1,0:T(8,128)(2,1)S(1)} %copy-done.2, ...), custom_call_target="tpu_custom_call" | custom-call | flops 100000000 | bytes 5000000 | tf_op jit(solution)/shard_map/pallas_call | solution.py:155
  101.8 12.8 %all_to_all.50 = f32[8,4,1152]{2,1,0:T(4,128)S(1)} all-to-all(f32[8,4,1152]{2,1,0:T(4,128)S(1)} %broadcast_in_dim.37), channel_id=1, replica_groups=mesh['ctx'=64,'cand'=8] {'cand'}, dimensions={0} | all-to-all | bytes 294912 | tf_op jit(solution)/shard_map/all_to_all | solution.py:53
  114.6 0.7 multiply_reduce_fusion.3
  115.4 0.4 fusion.41
  116.5 0.8 pad_maximum_fusion.7
  117.3 7.4 %all-to-all-start.6 = ((bf16[64,16,128]{2,1,0:T(8,128)(2,1)}), bf16[64,16,128]{2,1,0:T(8,128)(2,1)S(1)}, u32[]{:S(2)}, u32[]{:S(2)}) async-start(bf16[64,16,128]{2,1,0:T(8,128)(2,1)} %pad_maximum_fusion.7), calls=%async_computation.6 | async-start | bytes 524288 | tf_op jit(solution)/shard_map/all_to_all | solution.py:53
  124.8 12.4 %all-to-all-done.6 = bf16[64,16,128]{2,1,0:T(8,128)(2,1)S(1)} async-done(((bf16[64,16,128]{2,1,0:T(8,128)(2,1)}), bf16[64,16,128]{2,1,0:T(8,128)(2,1)S(1)}, u32[]{:S(2)}, u32[]{:S(2)}) %all-to-all-start.6) | async-done | bytes 262176 | tf_op jit(solution)/shard_map/all_to_all | solution.py:53
  138.1 0.4 convolution_convert_fusion
  138.7 1.0 pad_maximum_fusion
  139.6 5.3 %all-to-all-start.7 = ((bf16[64,40,128]{2,1,0:T(8,128)(2,1)}), bf16[64,40,128]{2,1,0:T(8,128)(2,1)S(1)}, u32[]{:S(2)}, u32[]{:S(2)}) async-start(bf16[64,40,128]{2,1,0:T(8,128)(2,1)} %pad_maximum_fusion), calls=%async_computation.8 | async-start | bytes 1310720 | tf_op jit(solution)/shard_map/all_to_all | solution.py:53
  145.1 1.4 fusion.73
  146.9 0.9 copy.98
  147.8 17.1 %all-to-all-done.7 = bf16[64,40,128]{2,1,0:T(8,128)(2,1)S(1)} async-done(((bf16[64,40,128]{2,1,0:T(8,128)(2,1)}), bf16[64,40,128]{2,1,0:T(8,128)(2,1)S(1)}, u32[]{:S(2)}, u32[]{:S(2)}) %all-to-all-start.7) | async-done | bytes 655392 | tf_op jit(solution)/shard_map/all_to_all | solution.py:53
  165.1 0.4 fusion.74
  165.5 0.7 multiply_bitcast_fusion.1
  166.2 3.3 %all-to-all-start.8 = ((f32[8,4,128]{2,1,0:T(4,128)}), f32[8,4,128]{2,1,0:T(4,128)S(1)}, u32[]{:S(2)}, u32[]{:S(2)}) async-start(f32[8,4,128]{2,1,0:T(4,128)} %multiply_bitcast_fusion.1), calls=%async_computation.9 | async-start | bytes 32768 | tf_op jit(solution)/shard_map/all_to_all | solution.py:53
  169.7 7.6 %all-to-all-done.8 = f32[8,4,128]{2,1,0:T(4,128)S(1)} async-done(((f32[8,4,128]{2,1,0:T(4,128)}), f32[8,4,128]{2,1,0:T(4,128)S(1)}, u32[]{:S(2)}, u32[]{:S(2)}) %all-to-all-start.8) | async-done | bytes 16416 | tf_op jit(solution)/shard_map/all_to_all | solution.py:53
  177.3 0.7 broadcast_in_dim.41
  178.0 6.5 %all-to-all-start.9 = ((bf16[64,8,128]{2,1,0:T(8,128)(2,1)}), bf16[64,8,128]{2,1,0:T(8,128)(2,1)S(1)}, u32[]{:S(2)}, u32[]{:S(2)}) async-start(bf16[64,8,128]{2,1,0:T(8,128)(2,1)} %broadcast_in_dim.41), calls=%async_computation.10 | async-start | bytes 262144 | tf_op jit(solution)/shard_map/all_to_all | solution.py:53
  184.5 0.6 dynamic-slice_bitcast_fusion
  185.1 9.7 %all-to-all-done.9 = bf16[64,8,128]{2,1,0:T(8,128)(2,1)S(1)} async-done(((bf16[64,8,128]{2,1,0:T(8,128)(2,1)}), bf16[64,8,128]{2,1,0:T(8,128)(2,1)S(1)}, u32[]{:S(2)}, u32[]{:S(2)}) %all-to-all-start.9) | async-done | bytes 131104 | tf_op jit(solution)/shard_map/all_to_all | solution.py:53
  195.1 0.6 pad_maximum_fusion.11
  195.7 1.8 convolution_add_fusion
  (134 shorter events, 4.8 us)
Async XLA Ops:
  7.2 19.0 %copy-start = (bf16[512,1024]{1,0:T(8,128)(2,1)S(1)}, bf16[512,1024]{1,0:T(8,128)(2,1)}, u32[]{:S(2)}) copy-start(bf16[512,1024]{1,0:T(8,128)(2,1)} %param.14) | copy-start | bytes 3145732
  7.2 47.8 %all-gather.6.cloned.1.call-start = ((), (), s32[]{:S(2)}) async-start(), calls=%async_computation.13 | async-start | bytes 1474560 | tf_op jit(solution)/shard_map/all_gather | solution.py:202
  9.1 17.1 %copy-start.29 = (bf16[1024,512]{1,0:T(8,128)(2,1)S(1)}, bf16[1024,512]{1,0:T(8,128)(2,1)}, u32[]{:S(2)}) copy-start(bf16[1024,512]{1,0:T(8,128)(2,1)} %param.16) | copy-start | bytes 3145732
  9.1 24.8 %all-to-all-start = ((bf16[64,4,128]{2,1,0:T(4,128)(2,1)}), bf16[64,4,128]{2,1,0:T(4,128)(2,1)S(1)}, u32[]{:S(2)}, u32[]{:S(2)}) async-start(bf16[64,4,128]{2,1,0:T(4,128)(2,1)} %bitcast.122), calls=%async_computation | async-start | bytes 131072 | tf_op jit(solution)/shard_map/all_to_all | solution.py:53
  24.1 70.7 %all-gather.4.cloned.1.call-start = ((), (), s32[]{:S(2)}) async-start(), calls=%async_computation.11 | async-start | bytes 2359296 | tf_op jit(solution)/shard_map/all_gather | solution.py:203
  26.1 22.7 %copy-start.7 = (bf16[1024,128]{1,0:T(8,128)(2,1)}, bf16[1024,128]{1,0:T(8,128)(2,1)S(1)}, u32[]{:S(2)}) copy-start(bf16[1024,128]{1,0:T(8,128)(2,1)S(1)} %get-tuple-element.42) | copy-start | bytes 786436
  26.2 22.7 %copy-start.9 = (bf16[1024,128]{1,0:T(8,128)(2,1)}, bf16[1024,128]{1,0:T(8,128)(2,1)S(1)}, u32[]{:S(2)}) copy-start(bf16[1024,128]{1,0:T(8,128)(2,1)S(1)} %get-tuple-element.43) | copy-start | bytes 786436
  26.2 31.1 %copy-start.11 = (bf16[1024,128]{1,0:T(8,128)(2,1)}, bf16[1024,128]{1,0:T(8,128)(2,1)S(1)}, u32[]{:S(2)}) copy-start(bf16[1024,128]{1,0:T(8,128)(2,1)S(1)} %get-tuple-element.41) | copy-start | bytes 786436
  26.2 31.1 %copy-start.12 = (bf16[1024,128]{1,0:T(8,128)(2,1)}, bf16[1024,128]{1,0:T(8,128)(2,1)S(1)}, u32[]{:S(2)}) copy-start(bf16[1024,128]{1,0:T(8,128)(2,1)S(1)} %get-tuple-element.44) | copy-start | bytes 786436
  26.2 1.6 copy-start.18
  26.2 1.5 copy-start.17
  27.7 37.1 %copy-start.21 = (f32[256]{0:T(256)}, f32[256]{0:T(256)S(1)}, u32[]{:S(2)}) copy-start(f32[256]{0:T(256)S(1)} %add_convert_fusion.1) | copy-start | bytes 3076
  34.6 13.9 %all-to-all-start.1 = ((bf16[8,4,128]{2,1,0:T(4,128)(2,1)}), bf16[8,4,128]{2,1,0:T(4,128)(2,1)S(1)}, u32[]{:S(2)}, u32[]{:S(2)}) async-start(bf16[8,4,128]{2,1,0:T(4,128)(2,1)} %broadcast_in_dim.31), calls=%async_computation.1 | async-start | bytes 16384 | tf_op jit(solution)/shard_map/all_to_all | solution.py:53
  40.8 24.0 %copy-start.26 = (s32[128]{0:T(128)}, s32[128]{0:T(128)S(1)}, u32[]{:S(2)}) copy-start(s32[128]{0:T(128)S(1)} %iota_add_fusion) | copy-start | bytes 1540
  49.7 15.1 %all-to-all-start.2 = ((bf16[64,4,128]{2,1,0:T(4,128)(2,1)}), bf16[64,4,128]{2,1,0:T(4,128)(2,1)S(1)}, u32[]{:S(2)}, u32[]{:S(2)}) async-start(bf16[64,4,128]{2,1,0:T(4,128)(2,1)} %broadcast_in_dim.32), calls=%async_computation.2 | async-start | bytes 131072 | tf_op jit(solution)/shard_map/all_to_all | solution.py:53
  57.3 8.4 %copy-start.23 = (f32[128]{0:T(128)}, f32[128]{0:T(128)S(1)}, u32[]{:S(2)}) copy-start(f32[128]{0:T(128)S(1)} %add_rsqrt_fusion.1) | copy-start | bytes 1540
  57.3 9.1 %copy-start.20 = (s32[4,512]{1,0:T(4,128)S(1)}, s32[4,512]{1,0:T(4,128)}, u32[]{:S(2)}) copy-start(s32[4,512]{1,0:T(4,128)} %param.20) | copy-start | bytes 24580
  58.6 13.1 %copy-start.13 = (bf16[128,256]{1,0:T(8,128)(2,1)}, bf16[128,256]{1,0:T(8,128)(2,1)S(1)}, u32[]{:S(2)}) copy-start(bf16[128,256]{1,0:T(8,128)(2,1)S(1)} %get-tuple-element.56) | copy-start | bytes 196612
  58.6 13.1 %copy-start.30 = (bf16[512,512]{1,0:T(8,128)(2,1)S(1)}, bf16[512,512]{1,0:T(8,128)(2,1)}, u32[]{:S(2)}) copy-start(bf16[512,512]{1,0:T(8,128)(2,1)} %fusion.3) | copy-start | bytes 1572868
  66.4 15.6 %all-to-all-start.3 = ((bf16[64,4,128]{2,1,0:T(4,128)(2,1)}), bf16[64,4,128]{2,1,0:T(4,128)(2,1)S(1)}, u32[]{:S(2)}, u32[]{:S(2)}) async-start(bf16[64,4,128]{2,1,0:T(4,128)(2,1)} %bitcast.9), calls=%async_computation.3 | async-start | bytes 131072 | tf_op jit(solution)/shard_map/all_to_all | solution.py:53
  71.6 2.6 %copy-start.4 = (bf16[1024,640]{1,0:T(8,128)(2,1)S(1)}, bf16[1024,640]{1,0:T(8,128)(2,1)}, u32[]{:S(2)}) copy-start(bf16[1024,640]{1,0:T(8,128)(2,1)} %all-gather.6.cloned.1.call-done) | copy-start | bytes 3932164
  74.2 12.8 %copy-start.19 = (s32[4,512]{1,0:T(4,128)S(1)}, s32[4,512]{1,0:T(4,128)}, u32[]{:S(2)}) copy-start(s32[4,512]{1,0:T(4,128)} %param.19) | copy-start | bytes 24580
  74.2 20.6 %copy-start.3 = (f32[512]{0:T(512)S(1)}, f32[512]{0:T(512)}, u32[]{:S(2)}) copy-start(f32[512]{0:T(512)} %param.17) | copy-start | bytes 6148
  83.1 11.7 %all-to-all-start.4 = ((bf16[8,16,128]{2,1,0:T(8,128)(2,1)}), bf16[8,16,128]{2,1,0:T(8,128)(2,1)S(1)}, u32[]{:S(2)}, u32[]{:S(2)}) async-start(bf16[8,16,128]{2,1,0:T(8,128)(2,1)} %broadcast_in_dim.34), calls=%async_computation.4 | async-start | bytes 65536 | tf_op jit(solution)/shard_map/all_to_all | solution.py:53
  94.8 1.6 copy-start.1
  96.4 1.6 copy-start.2
  101.8 14.1 %copy-start.6 = (bf16[128,1024]{1,0:T(8,128)(2,1)S(1)}, bf16[128,1024]{1,0:T(8,128)(2,1)}, u32[]{:S(2)}) copy-start(bf16[128,1024]{1,0:T(8,128)(2,1)} %param.13) | copy-start | bytes 786436
  115.9 21.6 %copy-start.14 = (bf16[128,256]{1,0:T(8,128)(2,1)S(1)}, bf16[128,256]{1,0:T(8,128)(2,1)}, u32[]{:S(2)}) copy-start(bf16[128,256]{1,0:T(8,128)(2,1)} %copy-done.13) | copy-start | bytes 196612
  115.9 21.6 %copy-start.22 = (f32[256]{0:T(256)S(1)}, f32[256]{0:T(256)}, u32[]{:S(2)}) copy-start(f32[256]{0:T(256)} %copy-done.21) | copy-start | bytes 3076
  115.9 21.6 %copy-start.27 = (s32[128]{0:T(128)S(1)}, s32[128]{0:T(128)}, u32[]{:S(2)}) copy-start(s32[128]{0:T(128)} %copy-done.26) | copy-start | bytes 1540
  115.9 21.6 %copy-start.31 = (f32[256,128]{1,0:T(8,128)S(1)}, f32[256,128]{1,0:T(8,128)}, u32[]{:S(2)}) copy-start(f32[256,128]{1,0:T(8,128)} %get-tuple-element.69) | copy-start | bytes 393220
  117.3 19.9 %all-to-all-start.6 = ((bf16[64,16,128]{2,1,0:T(8,128)(2,1)}), bf16[64,16,128]{2,1,0:T(8,128)(2,1)S(1)}, u32[]{:S(2)}, u32[]{:S(2)}) async-start(bf16[64,16,128]{2,1,0:T(8,128)(2,1)} %pad_maximum_fusion.7), calls=%async_computation.6 | async-start | bytes 524288 | tf_op jit(solution)/shard_map/all_to_all | solution.py:53
  124.7 13.4 %copy-start.5 = (bf16[1024,640]{1,0:T(8,128)(2,1)S(1)}, bf16[1024,640]{1,0:T(8,128)(2,1)}, u32[]{:S(2)}) copy-start(bf16[1024,640]{1,0:T(8,128)(2,1)} %all-gather.6.cloned.1.call-done) | copy-start | bytes 3932164
  124.7 13.4 %copy-start.24 = (f32[128]{0:T(128)S(1)}, f32[128]{0:T(128)}, u32[]{:S(2)}) copy-start(f32[128]{0:T(128)} %copy-done.23) | copy-start | bytes 1540
  137.9 0.6 copy-start.15
  138.6 6.4 %copy-start.16 = (bf16[128,128]{1,0:T(8,128)(2,1)S(1)}, bf16[128,128]{1,0:T(8,128)(2,1)}, u32[]{:S(2)}) copy-start(bf16[128,128]{1,0:T(8,128)(2,1)} %copy-done.15) | copy-start | bytes 98308
  138.7 6.4 %copy-start.25 = (f32[128]{0:T(128)S(1)}, f32[128]{0:T(128)}, u32[]{:S(2)}) copy-start(f32[128]{0:T(128)} %copy-done.23) | copy-start | bytes 1540
  139.6 25.3 %all-to-all-start.7 = ((bf16[64,40,128]{2,1,0:T(8,128)(2,1)}), bf16[64,40,128]{2,1,0:T(8,128)(2,1)S(1)}, u32[]{:S(2)}, u32[]{:S(2)}) async-start(bf16[64,40,128]{2,1,0:T(8,128)(2,1)} %pad_maximum_fusion), calls=%async_computation.8 | async-start | bytes 1310720 | tf_op jit(solution)/shard_map/all_to_all | solution.py:53
  145.0 50.8 %reduce-scatter.2.cloned.1.call-start = ((), (), s32[]{:S(2)}) async-start(), calls=%async_computation.12 | async-start | bytes 589824 | tf_op jit(solution)/shard_map/reduce_scatter | solution.py:325
  146.9 18.2 %copy-start.8 = (bf16[1024,128]{1,0:T(8,128)(2,1)S(1)}, bf16[1024,128]{1,0:T(8,128)(2,1)}, u32[]{:S(2)}) copy-start(bf16[1024,128]{1,0:T(8,128)(2,1)} %copy-done.7) | copy-start | bytes 786436
  146.9 18.2 %copy-start.10 = (bf16[1024,128]{1,0:T(8,128)(2,1)S(1)}, bf16[1024,128]{1,0:T(8,128)(2,1)}, u32[]{:S(2)}) copy-start(bf16[1024,128]{1,0:T(8,128)(2,1)} %copy-done.9) | copy-start | bytes 786436
  165.0 30.7 %copy-start.28 = (s32[128]{0:T(128)S(1)}, s32[128]{0:T(128)}, u32[]{:S(2)}) copy-start(s32[128]{0:T(128)} %copy-done.26) | copy-start | bytes 1540
  166.2 11.1 %all-to-all-start.8 = ((f32[8,4,128]{2,1,0:T(4,128)}), f32[8,4,128]{2,1,0:T(4,128)S(1)}, u32[]{:S(2)}, u32[]{:S(2)}) async-start(f32[8,4,128]{2,1,0:T(4,128)} %multiply_bitcast_fusion.1), calls=%async_computation.9 | async-start | bytes 32768 | tf_op jit(solution)/shard_map/all_to_all | solution.py:53
  178.0 16.9 %all-to-all-start.9 = ((bf16[64,8,128]{2,1,0:T(8,128)(2,1)}), bf16[64,8,128]{2,1,0:T(8,128)(2,1)S(1)}, u32[]{:S(2)}, u32[]{:S(2)}) async-start(bf16[64,8,128]{2,1,0:T(8,128)(2,1)} %broadcast_in_dim.41), calls=%async_computation.10 | async-start | bytes 262144 | tf_op jit(solution)/shard_map/all_to_all | solution.py:53
Sparse Core Ops, SparseCore 0:
  10.1 37.2 all-gather.5
  49.5 39.4 all-gather.3
  148.6 36.0 reduce-scatter.1
